TPU v7x, 32 devices: a whole 2x2x4 slice. The times are simulated.
32 devices in a mesh: ent: 16 (over z, y, x), rep: 2 (over core).
Axes of the slice: x: 2, y: 2, z: 4, core: 2. Of those that a mesh axis runs over, the one named last changes fastest.
Arguments:
- pieces: bfloat16 [4096, 8, 512], P(('ent', 'rep')), may hold values from -6 to 6
- lengths: int32 [4096], P(('ent', 'rep')), may hold values from 1 to 7
- scripts: int32 [4096], P(('ent', 'rep')), may hold values from 0 to 15
- script_table: float32 [16, 512], replicated, may hold values from -3 to 3
- gain_attn: float32 [512], replicated, may hold values from 0.5 to 1.5
- gain_ffn: float32 [512], replicated, may hold values from 0.5 to 1.5
- w_qkv: bfloat16 [512, 1536], replicated, may hold values from -0.25 to 0.25
- w_out: bfloat16 [512, 512], replicated, may hold values from -0.5 to 0.5
- w_up: bfloat16 [512, 2048], replicated, may hold values from -0.25 to 0.25
- w_down: bfloat16 [2048, 512], replicated, may hold values from -0.125 to 0.125
- w_proj: bfloat16 [512, 4096], P(None, 'ent'), may hold values from -0.25 to 0.25
- token_ids: int32 [8, 2048], P('rep'), may hold values from 0 to 4095
- out_grad: bfloat16 [4096, 8, 2048], P('ent', 'rep'), may hold values from -6 to 6
Outputs:
- looked_up: bfloat16 [4096, 8, 2048], P('ent', 'rep')
- grad_pieces: float32 [4096, 8, 512], P(('ent', 'rep'))
- grad_script_table: float32 [16, 512], replicated
- grad_gain_attn: float32 [512], replicated
- grad_gain_ffn: float32 [512], replicated
- grad_w_qkv: float32 [512, 1536], replicated
- grad_w_out: float32 [512, 512], replicated
- grad_w_up: float32 [512, 2048], replicated
- grad_w_down: float32 [2048, 512], replicated
- grad_w_proj: float32 [512, 4096], P(None, 'ent')
All inputs are finite; a program needn't handle non-finite values.
Results may differ from a plain program's by a relative error of at most 0.0074.
Values may be sent and summed in bfloat16 or wider, within the bound.
No kernel may reach another device: no remote copies, remote signals or barrier semaphores. Data moves between devices by JAX's collectives and lax.ppermute only.
A program may use at most 128 MiB of HBM per device.

v0:
```python
import functools
import math

import jax
import jax.numpy as jnp
import numpy as np
from jax import lax
from jax.experimental import pallas as pl
from jax.experimental.pallas import tpu as pltpu
from jax.sharding import PartitionSpec as P

HEADS = 8
HEAD_DIM = 64
F32 = jnp.float32
BF16 = jnp.bfloat16
highest = lax.Precision.HIGHEST
MIB = 1024 * 1024


def make_levels(ent_count, rep_count):
    levels = [("rep", rep_count, 0)]
    bit, total = 0, ent_count.bit_length() - 1
    while bit < total:
        width = 1 if bit < 2 else min(2, total - bit)
        levels.append(("ent", 1 << width, bit))
        bit += width
    return levels


def slot_of(number, levels):
    rep_count = levels[0][1]
    slot = number % rep_count
    ent = number // rep_count
    for _, size, shift in levels[1:]:
        slot = slot * size + (ent >> shift) % size
    return slot


def swap(value, level, k):
    name, size, shift = level
    count = lax.axis_size(name)
    return lax.ppermute(value, name, [(i, i ^ (k << shift)) for i in range(count)])


def merge(value):
    return value.reshape((-1,) + value.shape[-2:])


FAR = True


class Line:
    def __init__(self):
        self.last = []

    def run(self, body, name, micros, grid, ins, outs, prefetch=(), alias=None, room=24 * MIB, scratch=()):
        count = len(prefetch) + len(ins)
        extra = self.last + ([] if alias is None else [alias])
        token = (8, 128)

        def wrapped(*refs):
            held = len(refs) - len(scratch)
            refs[held - 1][...] = jnp.zeros(token, F32)
            body(*refs[:count], *refs[count + len(extra) : held - 1], *refs[held:])

        *results, last = pl.pallas_call(
            wrapped,
            grid_spec=pltpu.PrefetchScalarGridSpec(
                num_scalar_prefetch=len(prefetch),
                grid=grid,
                in_specs=[spec for _, spec in ins] + [pl.BlockSpec(memory_space=pl.ANY)] * len(extra),
                out_specs=[spec for _, _, spec, *_ in outs] + [pl.BlockSpec(token, lambda *_: (0, 0))],
                scratch_shapes=scratch,
            ),
            out_shape=[
                pltpu.HBM(shape, dtype) if far else jax.ShapeDtypeStruct(shape, dtype)
                for shape, dtype, _, *far in outs
            ]
            + [jax.ShapeDtypeStruct(token, F32)],
            input_output_aliases={} if alias is None else {count + len(extra) - 1: 0},
            compiler_params=pltpu.CompilerParams(vmem_limit_bytes=room),
            cost_estimate=pl.CostEstimate(
                flops=int(micros * 3e9), bytes_accessed=int(micros * 9e6), transcendentals=0
            ),
            name=name,
        )(*prefetch, *(value for value, _ in ins), *extra)
        self.last = [last]
        return results


def swap(value, level, k=1):
    name, size, shift = level
    count = lax.axis_size(name)
    return lax.ppermute(value, name, [(i, i ^ (k << shift)) for i in range(count)])


def swaps(values, level):
    return [swap(value, level, k) for k, value in enumerate(values, 1)]


ALL = slice(None)
BELOW = 16


def stage_body(layout, cuts, *refs):
    sums, position = [], 0
    for number in layout:
        sums.append(refs[position : position + number])
        position += number

    def piece(number, index, cols, rows=ALL):
        total = sums[number][0][index][rows, cols]
        for ref in sums[number][1:]:
            total = total.astype(F32) + ref[index][rows, cols].astype(F32)
        return total

    for out_ref, sources in zip(refs[position:], cuts):
        for target, parts in sources:
            for number, index, cols, row, col, *rows in parts:
                value = piece(number, index, cols, *rows).astype(out_ref.dtype)
                where = target + (slice(row, row + value.shape[0]), slice(col, col + value.shape[1]))
                out_ref[where] = value


def stage(line, sums, outs, steps=1):
    values = [value for kept, received in sums for value in [kept, *received]]

    def spec(shape):
        return pl.BlockSpec(memory_space=pltpu.VMEM)

    cuts = [
        [(target, source(target)) for target in np.ndindex(*lead)] for lead, _, _, _, source in outs
    ]
    shapes = [(lead + (rows, cols), dtype) for lead, rows, cols, dtype, _ in outs]
    held = [(value.shape, value.dtype) for value in values] + [(shape, jnp.dtype(dtype)) for shape, dtype in shapes]
    return line.run(
        functools.partial(stage_body, [1 + len(received) for _, received in sums], cuts),
        "exchange",
        0.5,
        (),
        [(value, spec(value.shape)) for value in values],
        [(shape, dtype, spec(shape)) for shape, dtype in shapes],
        room=2 * MIB + sum(math.prod(shape) * dtype.itemsize for shape, dtype in held),
    )


def split(number, value, axis, cols=ALL, width=None):
    lead = value.shape[:-2]
    rest = lead[:axis] + lead[axis + 1 :]
    outs = []
    for k in range(lead[axis]):

        def source(index, k=k):
            return [(number, index[:axis] + (k,) + index[axis:], cols, 0, 0)]

        outs.append((rest, value.shape[-2], width or value.shape[-1], F32 if k == 0 else BF16, source))
    return outs


def stacked(numbers, value, axis, rows=ALL):
    lead = value.shape[:-2]
    shape = lead[:axis] + (len(numbers),) + lead[axis:]

    def source(index):
        return [(numbers[index[axis]], index[:axis] + index[axis + 1 :], ALL, 0, 0)]

    return (shape, value.shape[-2], value.shape[-1], value.dtype, source)


def finish(line, sums, far, shape, dtype):
    whole = [(0, (), ALL, 0, 0)]
    for level in far:
        outs = [((), *shape, kind, lambda index: whole) for kind in (F32, BF16)]
        keep, send = stage(line, sums, outs)
        sums = [(keep, [swap(send, level, k) for k in range(1, level[1])])]
        yield
    yield stage(line, sums, [((), *shape, dtype, lambda index: whole)])[0]


def sum_halves(line, keep, send, levels, out, far=(), dtype=F32):
    received = swap(send, levels[0])
    yield
    rows, width = keep.shape[-2:]
    half = width // 2
    left, right = slice(0, half), slice(half, width)
    steps = 4 if rows % 64 == 0 else 1
    outs = split(0, keep, 0, left, half) + split(0, keep, 1, right, half)
    keep_a, send_a, keep_b, send_b = stage(line, [(keep, [received])], outs, steps)
    got_a, got_b = swap(send_a, levels[1]), swap(send_b, levels[2])
    yield
    outs = split(0, keep_a, 0) + split(1, keep_b, 0)
    sums = [(keep_a, [got_a]), (keep_b, [got_b])]
    keep_a, send_a, keep_b, send_b = stage(line, sums, outs, steps)
    sums = [(keep_a, [swap(send_a, levels[2])]), (keep_b, [swap(send_b, levels[1])])]
    yield
    for place, level in enumerate(levels[3:]):
        if place == 0:
            lead = keep_a.shape[1:-2]

            def source(index, k):
                return [(0, (k,) + index, ALL, 0, 0), (1, (k,) + index, ALL, 0, half)]

            outs = [
                (lead, rows, width, F32 if k == 0 else BF16, functools.partial(source, k=k))
                for k in range(level[1])
            ]
        else:
            outs = split(0, keep, 0)
        keep, *sends = stage(line, sums, outs)
        sums = [(keep, swaps(sends, level))]
        yield
    for value in finish(line, sums, far, (rows, width), dtype):
        if value is None:
            yield
    out.append(value)


def gather_halves(line, value, levels, out):
    rows, width = value.shape
    half = width // 2
    for place, level in reversed(list(enumerate(levels[3:]))):
        got = [swap(value, level, k) for k in range(1, level[1])]
        yield
        parts = [(part, []) for part in [value, *got]]
        numbers = list(range(level[1]))
        if place:
            value = stage(line, parts, [stacked(numbers, value, 0)])[0]
        else:
            lead = (level[1],) + value.shape[:-2]

            def source(index, cols):
                return [(index[0], index[1:], cols, 0, 0)]

            outs = [
                (lead, rows, half, BF16, functools.partial(source, cols=cols))
                for cols in (slice(0, half), slice(half, width))
            ]
            value_a, value_b = stage(line, parts, outs)
    got_a, got_b = swap(value_a, levels[2]), swap(value_b, levels[1])
    yield
    sums = [(part, []) for part in (value_a, got_a, value_b, got_b)]
    outs = [stacked([0, 1], value_a, 0), stacked([2, 3], value_b, 0)]
    value_a, value_b = stage(line, sums, outs)
    got_a, got_b = swap(value_a, levels[1]), swap(value_b, levels[2])
    yield
    sums = [(part, []) for part in (value_a, got_a, value_b, got_b)]
    lead = (2,) + value_a.shape[:-2]

    def joined(index):
        left, right = index[0], index[1]
        return [(left, index[1:], ALL, 0, 0), (2 + right, (left,) + index[2:], ALL, 0, half)]

    value = stage(line, sums, [(lead, rows, width, BF16, joined)])[0]
    out += [value, swap(value, levels[0])]
    yield


def all_sum(line, keep, send, near, far, out):
    mine = []
    yield from sum_halves(line, keep, send, near, mine, far, BF16)
    yield from gather_halves(line, mine[0], near, out)


def all_sum_two(line, keep_a, send_a, keep_b, send_b, extra, near, far, out):
    got_a, got_b = swap(send_a, near[0]), swap(send_b, near[0])
    yield
    rows = keep_a.shape[-2]
    outs = split(0, keep_a, 0) + split(1, keep_b, 1)
    keep_a, send_a, keep_b, send_b = stage(line, [(keep_a, [got_a]), (keep_b, [got_b])], outs)
    got_a, got_b = swap(send_a, near[1]), swap(send_b, near[2])
    yield
    outs = split(0, keep_a, 0) + split(1, keep_b, 0)
    keep_a, send_a, keep_b, send_b = stage(line, [(keep_a, [got_a]), (keep_b, [got_b])], outs)
    sums = [(keep_a, [swap(send_a, near[2])]), (keep_b, [swap(send_b, near[1])])]
    yield
    below = extra()
    added = below.shape[0]
    for place, level in enumerate(near[3:]):
        if place == 0:
            lead = keep_a.shape[1:-2]
            sums = sums + [(below, [])]

            def source(index, k):
                places = [(0, (k,) + index, 0), (1, (k,) + index, rows), (2, (), 2 * rows)]
                return [(number, where, ALL, row, 0) for number, where, row in places]

            outs = [
                (lead, 2 * rows + added, PANEL, F32 if k == 0 else BF16, functools.partial(source, k=k))
                for k in range(level[1])
            ]
        else:
            outs = split(0, keep, 0)
        keep, *sends = stage(line, sums, outs)
        sums = [(keep, swaps(sends, level))]
        yield
    for level in far:
        outs = [((), 2 * rows + added, PANEL, kind, lambda index: [(0, (), ALL, 0, 0)]) for kind in (F32, BF16)]
        keep, send = stage(line, sums, outs)
        sums = [(keep, [swap(send, level, k) for k in range(1, level[1])])]
        yield
    outs = [
        ((), size, PANEL, BF16, lambda index, part=part: [(0, (), ALL, 0, 0, part)])
        for size, part in ((2 * rows, slice(0, 2 * rows)), (added, slice(2 * rows, 2 * rows + added)))
    ]
    value, below = stage(line, sums, outs)
    for place, level in reversed(list(enumerate(near[3:]))):
        got = [swap(value, level, k) for k in range(1, level[1])]
        yield
        numbers = list(range(level[1]))
        parts = [(part, []) for part in [value, *got]]
        if place:
            value = stage(line, parts, [stacked(numbers, value, 0)])[0]
            continue
        lead = (level[1],) + value.shape[:-2]

        def first(index):
            return [(index[0], index[1:], ALL, 0, 0, slice(0, rows))]

        def second(index):
            number = int(np.ravel_multi_index(index, lead)) * BELOW % added
            return [
                (index[0], index[1:], ALL, 0, 0, slice(rows, 2 * rows)),
                (len(numbers), (), ALL, rows, 0, slice(number, number + BELOW)),
            ]

        outs = [(lead, rows, PANEL, BF16, first), (lead, rows + BELOW, PANEL, BF16, second)]
        value_a, value_b = stage(line, parts + [(below, [])], outs)
    got_a, got_b = swap(value_a, near[2]), swap(value_b, near[1])
    yield
    sums = [(part, []) for part in (value_a, got_a, value_b, got_b)]
    outs = [stacked([0, 1], value_a, 0), stacked([2, 3], value_b, 0)]
    value_a, value_b = stage(line, sums, outs)
    got_a, got_b = swap(value_a, near[1]), swap(value_b, near[2])
    yield
    sums = [(part, []) for part in (value_a, got_a, value_b, got_b)]
    outs = [stacked([0, 1], value_a, 0), stacked([2, 3], value_b, 1)]
    value_a, value_b = stage(line, sums, outs)
    out += [value_a, swap(value_a, near[0]), value_b, swap(value_b, near[0])]
    yield


def fixed(shape):
    return pl.BlockSpec(shape, lambda i, *_: (0,) * len(shape))


def rows_of(rows, width):
    return pl.BlockSpec((rows, width), lambda i, *_: (i, 0))


def selector(ids, base, rows):
    entry = lax.broadcasted_iota(jnp.int32, (rows, 1), 0).astype(jnp.int16)
    return jnp.where(entry == (ids - base).astype(jnp.int16), jnp.ones((), BF16), jnp.zeros((), BF16))


def nt(left, right):
    return lax.dot_general(left, right, (((1,), (1,)), ((), ())), preferred_element_type=F32)


def tn(left, right):
    return lax.dot_general(left, right, (((0,), (0,)), ((), ())), preferred_element_type=F32)


def mm(left, right):
    return jnp.dot(left, right, preferred_element_type=F32)


def scatter_body(first, ids_ref, grad_ref, proj_ref, table_ref, pooled_ref, flat_ref):
    @pl.when(pl.program_id(0) == 0)
    def _():
        flat_ref[...] = grad_ref[...].reshape(flat_ref.shape)

    rows = table_ref.shape[0]
    some = min(256, rows)
    parts = []
    for low in range(0, rows, some):
        base = first + pl.program_id(0) * rows + low
        picks = [selector(ids_ref[row : row + 1], base, some) for row in range(ids_ref.shape[0])]
        parts.append(nt(jnp.concatenate(picks, axis=1), flat_ref[...]))
    part = jnp.concatenate(parts, axis=0).astype(BF16)
    table_ref[...] = part
    pooled_ref[...] = nt(part, proj_ref[...]).astype(pooled_ref.dtype)


def scatter_rows(line, ids, grad, w_proj, first, count, dtype):
    features = grad.shape[0]
    width = w_proj.shape[0]
    rows = min(1024, count)
    return line.run(
        functools.partial(scatter_body, first),
        "scatter_rows",
        14,
        (count // rows,),
        [
            (ids, fixed(ids.shape)),
            (grad, pl.BlockSpec(memory_space=pltpu.VMEM)),
            (w_proj, fixed(w_proj.shape)),
        ],
        [
            ((count, features), BF16, rows_of(rows, features), FAR),
            ((count, width), dtype, rows_of(rows, width)),
        ],
        room=28 * MIB,
        scratch=[pltpu.VMEM((features, ids.size), BF16)],
    )


def table_body(steps, own_ref, other_ref, proj_ref, part_own_ref, part_other_ref, table_ref, grad_ref):
    step = pl.program_id(0)

    @pl.when(step == 0)
    def _():
        grad_ref[...] = jnp.zeros_like(grad_ref)

    def one(pooled_ref, part_ref):
        pooled = pooled_ref[...]
        cols = lax.dot_general(
            proj_ref[...], pooled, (((0,), (1,)), ((), ())), preferred_element_type=F32
        )
        table_ref[...] = cols.astype(BF16)
        grad_ref[...] += tn(pooled, part_ref[...])

    @pl.when(step < steps)
    def _():
        one(own_ref, part_own_ref)

    @pl.when(step >= steps)
    def _():
        one(other_ref, part_other_ref)


def table_and_grad(line, own, other, w_proj, part_own, part_other):
    count, width = own.shape
    features = w_proj.shape[1]
    rows = min(1024, count)
    steps = count // rows

    def first(cols):
        return pl.BlockSpec((rows, cols), lambda i, *_: (jnp.minimum(i, steps - 1), 0))

    def second(cols):
        return pl.BlockSpec((rows, cols), lambda i, *_: (jnp.maximum(i - steps, 0), 0))

    return line.run(
        functools.partial(table_body, steps),
        "table_and_grad",
        5,
        (2 * steps,),
        [
            (own, first(width)),
            (other, second(width)),
            (w_proj, fixed(w_proj.shape)),
            (part_own, first(features)),
            (part_other, second(features)),
        ],
        [
            ((features, 2 * count), BF16, pl.BlockSpec((features, rows), lambda i, *_: (0, i))),
            ((width, features), F32, fixed((width, features))),
        ],
    )


def lookup_body(chunk, ids_ref, *refs):
    table_refs, out_ref = refs[:-1], refs[-1]
    rows = ids_ref.shape[0]

    def find(base, table):
        picks = [selector(ids_ref[row : row + 1], base, chunk) for row in range(rows)]
        return mm(table, jnp.concatenate(picks, axis=1))

    total = None
    for index, table_ref in enumerate(table_refs):
        vocab = table_ref.shape[1]
        for inner in range(0, vocab, chunk):
            part = find(index * vocab + inner, table_ref[:, inner : inner + chunk])
            total = part if total is None else total + part
    out_ref[...] = total.astype(BF16).reshape(out_ref.shape)


def lookup(line, ids, tables, part, before=None):
    rows, text_len = ids.shape
    features, vocab = tables[0].shape
    block = text_len // 8
    first, last = part
    return line.run(
        functools.partial(lookup_body, min(vocab, 4096)),
        "lookup",
        3 * (last - first),
        (last - first,),
        [(ids, pl.BlockSpec((rows, block), lambda i, *_: (0, i + first)))]
        + [(table, fixed(table.shape)) for table in tables],
        [
            (
                (features, rows, text_len),
                BF16,
                pl.BlockSpec((features, rows, block), lambda i, *_: (0, 0, i + first)),
                FAR,
            )
        ],
        alias=before,
    )[0]


PANEL = 512


def store_slots(slots_ref, first, part, keep_ref, send_ref):
    half, rows, _ = keep_ref.shape
    for j in range(part.shape[0] // rows):
        slot = slots_ref[first + j]
        piece = part[j * rows : (j + 1) * rows]

        @pl.when(slot < half)
        def _():
            keep_ref[slot] = piece

        @pl.when(slot >= half)
        def _():
            send_ref[slot - half] = piece.astype(BF16)


def weight_body(slots_ref, left_ref, right_ref, keep_ref, send_ref):
    part = tn(left_ref[...], right_ref[...])
    store_slots(slots_ref, pl.program_id(0) * (part.shape[0] // keep_ref.shape[1]), part, keep_ref, send_ref)


def tall_body(steps, slots_ref, first_ref, second_ref, right_ref, keep_ref, send_ref):
    step = pl.program_id(0)
    each = PANEL // keep_ref.shape[1]

    @pl.when(step < steps)
    def _():
        store_slots(slots_ref, step * each, tn(first_ref[...], right_ref[...]), keep_ref, send_ref)

    @pl.when(step >= steps)
    def _():
        store_slots(slots_ref, step * each, tn(second_ref[...], right_ref[...]), keep_ref, send_ref)


def two_weights_body(last, slots_ref, left_ref, right_ref, left2_ref, right2_ref, keep_ref, send_ref):
    step = pl.program_id(0)
    each = left_ref.shape[1] // keep_ref.shape[1]

    @pl.when(step < last)
    def _():
        store_slots(slots_ref, step * each, tn(left_ref[...], right_ref[...]), keep_ref, send_ref)

    @pl.when(step == last)
    def _():
        store_slots(slots_ref, step * each, tn(left2_ref[...], right2_ref[...]), keep_ref, send_ref)


def slot_outs(count, rows):
    shape = (count // 2, rows, PANEL)
    return [(shape, F32, fixed(shape)), (shape, BF16, fixed(shape))]


def panel_of(depth):
    return pl.BlockSpec((depth, PANEL), lambda i, *_: (0, i))


def tall_weight(line, slots, lefts, right):
    depth, half = lefts[0].shape
    steps = half // PANEL
    return line.run(
        functools.partial(tall_body, steps),
        "tall_weight",
        3,
        (2 * steps,),
        [
            (lefts[0], pl.BlockSpec((depth, PANEL), lambda i, *_: (0, jnp.minimum(i, steps - 1)))),
            (lefts[1], pl.BlockSpec((depth, PANEL), lambda i, *_: (0, jnp.maximum(i - steps, 0)))),
            (right, fixed(right.shape)),
        ],
        slot_outs(slots.shape[0], 2 * half // slots.shape[0]),
        [slots],
    )


def wide_weight(line, slots, left, right):
    depth, cols = right.shape
    return line.run(
        weight_body,
        "wide_weight",
        8,
        (cols // PANEL,),
        [(left, fixed(left.shape)), (right, panel_of(depth))],
        slot_outs(slots.shape[0], cols // PANEL * left.shape[1] // slots.shape[0]),
        [slots],
    )


def two_weights(line, slots, left, right, left2, right2):
    depth, cols = right.shape
    last = cols // PANEL
    return line.run(
        functools.partial(two_weights_body, last),
        "two_weights",
        5,
        (last + 1,),
        [
            (left, fixed(left.shape)),
            (right, pl.BlockSpec((depth, PANEL), lambda i, *_: (0, jnp.minimum(i, last - 1)))),
            (left2, fixed(left2.shape)),
            (right2, fixed(right2.shape)),
        ],
        slot_outs(slots.shape[0], (last + 1) * left.shape[1] // slots.shape[0]),
        [slots],
    )


def load_slots(slots_ref, first, own_ref, other_ref, out_ref, rows):
    half = own_ref.shape[0]
    for j in range(out_ref.shape[0] // rows):
        slot = slots_ref[first + j]

        @pl.when(slot < half)
        def _():
            out_ref[j * rows : (j + 1) * rows] = own_ref[slot, :rows].astype(F32)

        @pl.when(slot >= half)
        def _():
            out_ref[j * rows : (j + 1) * rows] = other_ref[slot - half, :rows].astype(F32)


def unpack_body(slots_ref, own_ref, other_ref, out_ref):
    rows = own_ref.shape[1]
    each = out_ref.shape[0] // rows
    load_slots(slots_ref, pl.program_id(0) * each, own_ref, other_ref, out_ref, rows)


def unpack(line, slots, own, other, height):
    tile = min(512, height)
    return line.run(
        unpack_body,
        "unpack",
        5,
        (height // tile,),
        [(own, fixed(own.shape)), (other, fixed(other.shape))],
        [((height, PANEL), F32, pl.BlockSpec((tile, PANEL), lambda i, *_: (i, 0)), FAR)],
        [slots],
    )[0]


def unpack_extra_body(rows, inner, slots_ref, own_ref, other_ref, out_ref, *extra_refs):
    each = out_ref.shape[0] // rows
    load_slots(slots_ref, pl.program_id(0) * each, own_ref, other_ref, out_ref, rows)

    @pl.when(pl.program_id(0) == 0)
    def _():
        needed = sum(ref.shape[0] for ref in extra_refs)
        sums = []
        for place in range((needed + BELOW - 1) // BELOW):
            total = jnp.zeros((BELOW, PANEL), F32)
            for ref in (own_ref, other_ref):
                for slot in range(place, ref.shape[0], inner):
                    total += ref[slot, rows:].astype(F32)
            sums.append(total)
        total = jnp.concatenate(sums, axis=0)
        first = 0
        for ref in extra_refs:
            ref[...] = total[first : first + ref.shape[0]]
            first += ref.shape[0]


def unpack_extra(line, slots, own, other, height, cols, extra, inner):
    return line.run(
        functools.partial(unpack_extra_body, height * cols // PANEL // slots.shape[0], inner),
        "unpack",
        5,
        (cols // PANEL,),
        [(own, fixed(own.shape)), (other, fixed(other.shape))],
        [((height, cols), F32, pl.BlockSpec((height, PANEL), lambda i, *_: (0, i)), FAR)]
        + [((rows, PANEL), F32, fixed((rows, PANEL))) for rows in extra],
        [slots],
    )


def unpack_two_body(last, slots_ref, own_ref, other_ref, out_ref, out2_ref):
    step = pl.program_id(0)
    rows = own_ref.shape[1]
    each = out_ref.shape[0] // rows

    @pl.when(step < last)
    def _():
        load_slots(slots_ref, step * each, own_ref, other_ref, out_ref, rows)

    @pl.when(step == last)
    def _():
        load_slots(slots_ref, step * each, own_ref, other_ref, out2_ref, rows)


def unpack_two(line, slots, own, other, height, cols):
    last = cols // PANEL
    return line.run(
        functools.partial(unpack_two_body, last),
        "unpack_two",
        5,
        (last + 1,),
        [(own, fixed(own.shape)), (other, fixed(other.shape))],
        [
            (
                (height, cols),
                F32,
                pl.BlockSpec((height, PANEL), lambda i, *_: (0, jnp.minimum(i, last - 1))),
                FAR,
            ),
            ((height, PANEL), F32, fixed((height, PANEL)), FAR),
        ],
        [slots],
    )


GROUP = 128
PAIR = 2 * HEAD_DIM
GELU_SCALE = 0.7978845608028654
GELU_CUBE = 0.044715


def center(values):
    centered = values - jnp.mean(values, axis=-1, keepdims=True)
    spread = jnp.mean(centered * centered, axis=-1, keepdims=True)
    rate = lax.rsqrt(spread + 1e-05)
    return centered * rate, rate


def center_back(grad, gain, unit, rate):
    gain_grad = jnp.sum(grad * unit, axis=0, keepdims=True)
    grad = grad * gain
    mean_grad = jnp.mean(grad, axis=-1, keepdims=True)
    mean_unit = jnp.mean(grad * unit, axis=-1, keepdims=True)
    return rate * (grad - mean_grad - unit * mean_unit), gain_grad


def start_of(pieces_ref, scripts_ref, script_table_ref):
    entries, slots, width = pieces_ref.shape
    groups = script_table_ref.shape[0]
    pieces = pieces_ref[...].astype(F32).reshape(entries * slots, width)
    onehot = (scripts_ref[...] == lax.broadcasted_iota(jnp.int32, (1, groups), 1)).astype(F32)
    return pieces + jnp.dot(onehot, script_table_ref[...], precision=highest), onehot


def slot_weights(lengths, slots):
    rows = lengths.shape[0]
    slot = lax.broadcasted_iota(jnp.int32, (rows, 1), 0) % slots
    return jnp.where(slot <= lengths, 1.0 / (lengths + 1).astype(F32), 0.0)


def split_heads(pair):
    first = lax.broadcasted_iota(jnp.int32, pair.shape, 1) < HEAD_DIM
    zero = jnp.zeros_like(pair)
    return jnp.concatenate([jnp.where(first, pair, zero), jnp.where(first, zero, pair)], axis=0)


def join_heads(stacked):
    first = lax.broadcasted_iota(jnp.int32, (GROUP, PAIR), 1) < HEAD_DIM
    return jnp.where(first, stacked[:GROUP], stacked[GROUP:])


def attn_body(
    slots,
    pieces_ref,
    scripts_ref,
    lengths_ref,
    script_table_ref,
    gain_attn_ref,
    gain_ffn_ref,
    w_qkv_ref,
    w_out_ref,
    normed_ref,
    mixed_ref,
    context_ref,
    middle_ref,
    normed_ffn_ref,
):
    start, _ = start_of(pieces_ref, scripts_ref, script_table_ref)
    rows, width = start.shape
    lengths = lengths_ref[...]
    normed = (center(start)[0] * gain_attn_ref[...]).astype(BF16)
    normed_ref[...] = normed
    mixed = mm(normed, w_qkv_ref[...]).astype(BF16)
    mixed_ref[...] = mixed
    row = lax.broadcasted_iota(jnp.int32, (GROUP, GROUP), 0)
    col = lax.broadcasted_iota(jnp.int32, (GROUP, GROUP), 1)
    groups = []
    for base in range(0, rows, GROUP):
        part = mixed[base : base + GROUP]
        valid = (row // slots == col // slots) & (col % slots <= lengths[base : base + GROUP])
        lows = range(0, width, PAIR)
        raws = [
            nt(part[:, low : low + PAIR], split_heads(part[:, width + low : width + low + PAIR]))
            for low in lows
        ]
        heads = [raw[:, side : side + GROUP] for raw in raws for side in (0, GROUP)]
        heads = [jnp.where(valid, head * HEAD_DIM ** (-0.5), -1000000000.0) for head in heads]
        heads = [jnp.exp(head - jnp.max(head, axis=1, keepdims=True)) for head in heads]
        heads = [(head * (1.0 / jnp.sum(head, axis=1, keepdims=True))).astype(BF16) for head in heads]
        pairs = [
            mm(
                jnp.concatenate(heads[2 * j : 2 * j + 2], axis=1),
                split_heads(part[:, 2 * width + low : 2 * width + low + PAIR]),
            )
            for j, low in enumerate(lows)
        ]
        groups.append(jnp.concatenate(pairs, axis=1).astype(BF16))
    context = jnp.concatenate(groups, axis=0)
    context_ref[...] = context
    middle = start + mm(context, w_out_ref[...])
    middle_ref[...] = middle
    normed_ffn_ref[...] = (center(middle)[0] * gain_ffn_ref[...]).astype(BF16)


def attn_forward(
    line, pieces, scripts, lengths, script_table, gain_attn, gain_ffn, w_qkv, w_out
):
    entries, slots, width = pieces.shape
    total = entries * slots
    rows = math.gcd(total, 256)
    some = rows // slots
    whole = (script_table, gain_attn, gain_ffn, w_qkv, w_out)
    return line.run(
        functools.partial(attn_body, slots),
        "attn_forward",
        12,
        (total // rows,),
        [
            (pieces, pl.BlockSpec((some, slots, width), lambda i, *_: (i, 0, 0))),
            (scripts, rows_of(rows, 1)),
            (lengths, rows_of(rows, 1)),
        ]
        + [(value, fixed(value.shape)) for value in whole],
        [
            ((total, width), BF16, rows_of(rows, width)),
            ((total, 3 * width), BF16, rows_of(rows, 3 * width), FAR),
            ((total, width), BF16, rows_of(rows, width)),
            ((total, width), F32, rows_of(rows, width)),
            ((total, width), BF16, rows_of(rows, width)),
        ],
    )


def ffn_body(
    slots,
    last,
    length_rows_ref,
    lengths_ref,
    before_ref,
    normed_ref,
    w_up_ref,
    w_down_ref,
    slope_ref,
    hidden_ref,
    pooled_ref,
):
    rows, width = normed_ref.shape
    some = rows // slots
    row = lax.broadcasted_iota(jnp.int32, (some, rows), 1)
    entry = lax.broadcasted_iota(jnp.int32, (some, rows), 0)
    lengths = lengths_ref[...]
    valid = (row // slots == entry) & (row % slots <= lengths)
    valid = jnp.where(valid, 1.0, 0.0).astype(BF16)
    scale = 1.0 / (lengths + 1).astype(F32)
    pooled = before_ref[...]
    if not last:
        weights = slot_weights(length_rows_ref[...], slots)
        pooled = jnp.sum((pooled * weights).reshape(some, slots, width), axis=1)
    ff = w_up_ref.shape[1]
    step = ff // 2
    for low in range(0, ff, step):
        up = mm(normed_ref[...], w_up_ref[:, low : low + step])
        square = up * up
        tanh = jnp.tanh(up * (GELU_SCALE + GELU_SCALE * GELU_CUBE * square))
        half_up = 0.5 * up
        hidden = (half_up + half_up * tanh).astype(BF16)
        slope_ref[:, low : low + step] = (0.5 + 0.5 * tanh) + half_up * (1.0 - tanh * tanh) * (
            GELU_SCALE + 3.0 * GELU_SCALE * GELU_CUBE * square
        )
        mean_hidden = mm(valid, hidden) * scale
        high = mean_hidden.astype(BF16)
        rest = (mean_hidden - high.astype(F32)).astype(BF16)
        hidden_ref[:, low : low + step] = high
        w_down = w_down_ref[low : low + step]
        pooled += mm(high, w_down) + mm(rest, w_down)
    pooled_ref[...] = pooled.astype(pooled_ref.dtype)


def ffn_forward(line, length_rows, lengths, before, normed, w_up, w_down, last):
    total, width = normed.shape
    entries = lengths.shape[0]
    slots = total // entries
    rows = math.gcd(total, 256)
    some = rows // slots
    ff = w_up.shape[1] // 2
    return line.run(
        functools.partial(ffn_body, slots, last),
        "ffn_forward",
        7,
        (total // rows,),
        [
            (length_rows, rows_of(rows, 1)),
            (lengths, rows_of(some, 1)),
            (before, rows_of(some if last else rows, width)),
            (normed, rows_of(rows, width)),
            (w_up, pl.BlockSpec((width, ff), lambda i, *_: (0, int(last)))),
            (w_down, pl.BlockSpec((ff, width), lambda i, *_: (int(last), 0))),
        ],
        [
            ((total, ff), F32, rows_of(rows, ff), FAR),
            ((entries, ff), BF16, rows_of(some, ff)),
            ((entries, width), BF16 if last else F32, rows_of(some, width)),
        ],
    )


def ffn_back_body(
    slots,
    pooled_grad_ref,
    lengths_ref,
    slope_a_ref,
    slope_b_ref,
    middle_ref,
    gain_ffn_ref,
    w_up_ref,
    w_down_ref,
    grad_up_ref,
    grad_middle_ref,
    grad_branch_ref,
    gain_grad_ref,
):
    pooled_grad = pooled_grad_ref[...]
    rows, width = middle_ref.shape
    some = rows // slots
    wide = jnp.broadcast_to(pooled_grad[:, None, :], (some, slots, width)).reshape(rows, width)
    grad_final = wide * slot_weights(lengths_ref[...], slots)
    grad_ffn = grad_final.astype(BF16)
    ff = w_up_ref.shape[1]
    step = ff // 4
    grad_normed = jnp.zeros((rows, width), F32)
    for low in range(0, ff, step):
        grad_hidden = nt(grad_ffn, w_down_ref[low : low + step])
        slope_ref, inner = (slope_a_ref, low) if low < ff // 2 else (slope_b_ref, low - ff // 2)
        grad_up = (slope_ref[:, inner : inner + step] * grad_hidden).astype(BF16)
        grad_up_ref[:, low : low + step] = grad_up
        grad_normed += nt(grad_up, w_up_ref[:, low : low + step])
    unit, rate = center(middle_ref[...])
    grad, gain_grad = center_back(grad_normed, gain_ffn_ref[...], unit, rate)
    grad_middle = grad_final + grad
    grad_middle_ref[...] = grad_middle
    grad_branch_ref[...] = grad_middle.astype(BF16)

    @pl.when(pl.program_id(0) == 0)
    def _():
        gain_grad_ref[...] = jnp.zeros_like(gain_grad_ref)

    gain_grad_ref[...] += gain_grad


def ffn_back(line, pooled_grad, lengths, slopes, middle, gain_ffn, w_up, w_down):
    total, width = middle.shape
    entries = pooled_grad.shape[0]
    slots = total // entries
    rows = math.gcd(total, 256)
    some = rows // slots
    ff = w_up.shape[1]
    return line.run(
        functools.partial(ffn_back_body, slots),
        "ffn_back",
        15,
        (total // rows,),
        [
            (pooled_grad, rows_of(some, width)),
            (lengths, rows_of(rows, 1)),
            *((slope, rows_of(rows, ff // 2)) for slope in slopes),
            (middle, rows_of(rows, width)),
            (gain_ffn, fixed(gain_ffn.shape)),
            (w_up, fixed(w_up.shape)),
            (w_down, fixed(w_down.shape)),
        ],
        [
            ((total, ff), BF16, rows_of(rows, ff)),
            ((total, width), F32, rows_of(rows, width)),
            ((total, width), BF16, rows_of(rows, width)),
            ((1, width), F32, fixed((1, width))),
        ],
    )


def heads_back_body(slots, lengths_ref, w_out_ref, mixed_ref, grad_branch_ref, grad_mixed_ref):
    rows, width = grad_branch_ref.shape
    lengths = lengths_ref[...]
    grad_ctx = nt(grad_branch_ref[...], w_out_ref[...]).astype(BF16)
    row = lax.broadcasted_iota(jnp.int32, (GROUP, GROUP), 0)
    col = lax.broadcasted_iota(jnp.int32, (GROUP, GROUP), 1)
    same = row // slots == col // slots
    lows = range(0, width, PAIR)
    for base in range(0, rows, GROUP):
        span = slice(base, base + GROUP)
        valid = same & (row % slots <= lengths[span])
        queries = [mixed_ref[span, low : low + PAIR] for low in lows]
        keys = [split_heads(mixed_ref[span, width + low : width + low + PAIR]) for low in lows]
        values = [split_heads(mixed_ref[span, 2 * width + low : 2 * width + low + PAIR]) for low in lows]
        grad_pairs = [grad_ctx[span, low : low + PAIR] for low in lows]
        raws = [nt(key, query) for key, query in zip(keys, queries)]
        grad_raws = [nt(value, grad_pair) for value, grad_pair in zip(values, grad_pairs)]
        sides = (slice(0, GROUP), slice(GROUP, 2 * GROUP))
        heads = [raw[side] for raw in raws for side in sides]
        heads = [jnp.where(valid, head * HEAD_DIM ** (-0.5), -1000000000.0) for head in heads]
        heads = [jnp.exp(head - jnp.max(head, axis=0, keepdims=True)) for head in heads]
        probs = [head * (1.0 / jnp.sum(head, axis=0, keepdims=True)) for head in heads]
        grads = [grad_raw[side] for grad_raw in grad_raws for side in sides]
        grads = [
            prob * (grad - jnp.sum(grad * prob, axis=0, keepdims=True)) for prob, grad in zip(probs, grads)
        ]
        probs = [prob.astype(BF16) for prob in probs]
        grads = [(grad * HEAD_DIM ** (-0.5)).astype(BF16) for grad in grads]
        for j, low in enumerate(lows):
            scores_grad = jnp.concatenate(grads[2 * j : 2 * j + 2], axis=0)
            prob = jnp.concatenate(probs[2 * j : 2 * j + 2], axis=0)
            grad_mixed_ref[span, low : low + PAIR] = tn(scores_grad, keys[j]).astype(BF16)
            grad_keys = join_heads(mm(scores_grad, queries[j]))
            grad_mixed_ref[span, width + low : width + low + PAIR] = grad_keys.astype(BF16)
            grad_values = join_heads(mm(prob, grad_pairs[j]))
            grad_mixed_ref[span, 2 * width + low : 2 * width + low + PAIR] = grad_values.astype(BF16)


def heads_back(line, lengths, w_out, mixed, grad_branch, slots):
    total, width = grad_branch.shape
    rows = math.gcd(total, 256)
    return line.run(
        functools.partial(heads_back_body, slots),
        "heads_back",
        13,
        (total // rows,),
        [
            (lengths, rows_of(rows, 1)),
            (w_out, fixed(w_out.shape)),
            (mixed, rows_of(rows, 3 * width)),
            (grad_branch, rows_of(rows, width)),
        ],
        [((total, 3 * width), BF16, rows_of(rows, 3 * width))],
    )[0]


def attn_back_body(
    pieces_ref,
    scripts_ref,
    script_table_ref,
    gain_attn_ref,
    w_qkv_ref,
    grad_mixed_ref,
    grad_middle_ref,
    gain_ffn_grad_ref,
    grad_pieces_ref,
    small_ref,
):
    start, onehot = start_of(pieces_ref, scripts_ref, script_table_ref)
    grad_normed = nt(grad_mixed_ref[...], w_qkv_ref[...])
    unit, rate = center(start)
    grad, gain_grad = center_back(grad_normed, gain_attn_ref[...], unit, rate)
    grad_pieces = grad_middle_ref[...] + grad
    grad_pieces_ref[...] = grad_pieces.reshape(grad_pieces_ref.shape)

    groups = onehot.shape[1]

    @pl.when(pl.program_id(0) == 0)
    def _():
        small_ref[...] = jnp.zeros_like(small_ref)
        small_ref[groups + 1 : groups + 2] = gain_ffn_grad_ref[...]

    small_ref[groups : groups + 1] += gain_grad
    small_ref[:groups] += lax.dot_general(
        onehot, grad_pieces, (((0,), (0,)), ((), ())), precision=highest
    )


def attn_back(
    line, pieces, scripts, script_table, gain_attn, w_qkv, grad_mixed, grad_middle, gain_ffn_grad
):
    entries, slots, width = pieces.shape
    total = entries * slots
    rows = math.gcd(total, 256)
    some = rows // slots
    small = ((script_table.shape[0] + 2 + 15) // 16 * 16, width)
    return line.run(
        attn_back_body,
        "attn_back",
        9,
        (total // rows,),
        [
            (pieces, pl.BlockSpec((some, slots, width), lambda i, *_: (i, 0, 0))),
            (scripts, rows_of(rows, 1)),
            (script_table, fixed(script_table.shape)),
            (gain_attn, fixed(gain_attn.shape)),
            (w_qkv, fixed(w_qkv.shape)),
            (grad_mixed, rows_of(rows, 3 * width)),
            (grad_middle, rows_of(rows, width)),
            (gain_ffn_grad, fixed(gain_ffn_grad.shape)),
        ],
        [
            ((entries, slots, width), F32, pl.BlockSpec((some, slots, width), lambda i, *_: (i, 0, 0)), FAR),
            (small, F32, fixed(small)),
        ],
    )


PLAN = ("f t T f", "03 t f", "36 t f", "68 t f t", "w t E F", "Q")


def per_device(
    pieces,
    lengths,
    scripts,
    script_table,
    gain_attn,
    gain_ffn,
    w_qkv,
    w_out,
    w_up,
    w_down,
    w_proj,
    token_ids,
    out_grad,
):
    entries, slots, width = pieces.shape
    ent_count = lax.axis_size("ent")
    rep_count = lax.axis_size("rep")
    devices = ent_count * rep_count
    features = w_proj.shape[1]
    vocab = entries * devices
    rows_dev, text_len = token_ids.shape
    tokens = rows_dev * text_len
    levels = make_levels(ent_count, rep_count)
    sizes = tuple(size for _, size, _ in levels)
    me = lax.axis_index("ent") * rep_count + lax.axis_index("rep")
    chunks = 1 if devices <= 32 else 8
    each = entries // chunks
    span = vocab // chunks
    slot = slot_of(token_ids // entries ^ me, levels)
    within = token_ids % entries
    slot_ids = within // each * span + slot * each + within % each
    script_rows = jnp.repeat(scripts, slots)[:, None]
    length_rows = jnp.repeat(lengths, slots)[:, None]
    gain_attn, gain_ffn = gain_attn[None], gain_ffn[None]

    cut = len(levels)
    while math.prod(sizes[:cut]) * 16 > w_down.shape[0]:
        cut -= 1
    near, far = levels[:cut], levels[cut:]
    count = math.prod(sizes[:cut])
    slot_index = jnp.arange(count, dtype=jnp.int32) ^ slot_of(me, near)
    line = Line()

    def cut_up(keep, send, some):
        shape = tuple(size for _, size, _ in some[1:]) + keep.shape[-2:]
        return keep.reshape(shape), send.reshape(shape)

    parts, pooled_grads = [], []
    for chunk in range(chunks):
        first = chunk * span
        part_send, send = scatter_rows(
            line, slot_ids, out_grad, w_proj, first + span // 2, span // 2, BF16
        )
        part_keep, keep = scatter_rows(line, slot_ids, out_grad, w_proj, first, span // 2, F32)
        parts.append((part_keep, part_send))
        shape = sizes[1:] + (each, width)
        pooling = sum_halves(line, keep.reshape(shape), send.reshape(shape), levels, pooled_grads)
        if chunks > 1:
            for _ in pooling:
                pass
    next(pooling, None)
    next(pooling, None)
    normed, mixed, context, middle, normed_ffn = attn_forward(
        line, pieces, script_rows, length_rows, script_table, gain_attn, gain_ffn, w_qkv, w_out
    )
    next(pooling, None)
    length_cols = lengths[:, None]
    slope_a, hidden_a, pooled = ffn_forward(
        line, length_rows, length_cols, middle, normed_ffn, w_up, w_down, False
    )
    next(pooling, None)
    slope_b, hidden_b, pooled = ffn_forward(
        line, length_rows, length_cols, pooled, normed_ffn, w_up, w_down, True
    )
    for _ in pooling:
        pass
    grad_pooled = jnp.concatenate(pooled_grads, axis=0) if chunks > 1 else pooled_grads[0]

    held = [((), each, width, BF16, lambda index: [(0, (), ALL, 0, 0)])]
    halves = [[] for _ in range(chunks)]
    spreads = [
        gather_halves(
            line, stage(line, [(pooled[chunk * each :][:each], [])], held)[0], levels, halves[chunk]
        )
        for chunk in range(chunks)
    ]

    def spread_on():
        if chunks == 1:
            next(spreads[0])

    spread_on()
    down = tall_weight(line, slot_index, (hidden_a, hidden_b), grad_pooled.astype(BF16))
    grad_up, grad_middle, grad_branch, part_gain_ffn = ffn_back(
        line, grad_pooled, length_rows, (slope_a, slope_b), middle, gain_ffn, w_up, w_down
    )
    spread_on()
    up = wide_weight(line, slot_index, normed_ffn, grad_up)
    small, ffn_all, two_all = [], [], []
    ffn_sum = all_sum_two(
        line, *cut_up(*down, near), *cut_up(*up, near), lambda: small[0], near, far, ffn_all
    )
    next(ffn_sum)
    spread_on()
    grad_mixed = heads_back(line, length_rows, w_out, mixed, grad_branch, slots)
    next(ffn_sum)
    two = two_weights(line, slot_index, normed, grad_mixed, context, grad_branch)
    two_sum = all_sum(line, *cut_up(*two, near), near, far, two_all)
    next(two_sum)
    spread_on()
    grad_pieces, part_small = attn_back(
        line,
        pieces,
        script_rows,
        script_table,
        gain_attn,
        w_qkv,
        grad_mixed,
        grad_middle,
        part_gain_ffn,
    )
    small.append(part_small)
    results = {}

    def make_table():
        tables, total = [], None
        for chunk in range(chunks):
            for _ in spreads[chunk]:
                pass
            own, other = (value.reshape(span // 2, width) for value in halves[chunk])
            table, part = table_and_grad(line, own, other, w_proj, *parts[chunk])
            tables.append(table)
            total = part if total is None else total + part
        results["tables"] = tables
        results["proj"] = total, swap(total, levels[0])

    def look_up(first, last):
        before = results.get("looked_up")
        results["looked_up"] = lookup(line, slot_ids, results["tables"], (first, last), before)

    def add_proj():
        total, other = results["proj"]
        whole = [((), width, features, F32, lambda index: [(0, (), ALL, 0, 0)])]
        results["w_proj"] = stage(line, [(total, [other])], whole)[0]

    def end_ffn():
        results["w_down"] = unpack(line, slot_index, *map(merge, ffn_all[:2]), w_down.shape[0])
        results["w_up"], *results["small"] = unpack_extra(
            line,
            slot_index,
            *map(merge, ffn_all[2:]),
            *w_up.shape,
            (script_table.shape[0], 1, 1),
            math.prod(sizes[3:cut]),
        )

    def end_two():
        for _ in two_sum:
            pass
        results["w_qkv"], results["w_out"] = unpack_two(
            line, slot_index, *map(merge, two_all), *w_qkv.shape
        )

    acts = {
        "f": lambda: next(ffn_sum, 0),
        "t": lambda: next(two_sum, 0),
        "T": make_table,
        "w": add_proj,
        "E": lambda: list(ffn_sum),
        "F": end_ffn,
        "Q": end_two,
    }
    for act in (act for part in PLAN for act in part.split()):
        if act.isdigit():
            look_up(int(act[0]), int(act[1]))
        else:
            acts[act]()
    looked_up, grad_w_proj = results["looked_up"], results["w_proj"]
    grad_w_down, grad_w_up = results["w_down"], results["w_up"]
    grad_w_qkv, grad_w_out = results["w_qkv"], results["w_out"]
    grad_script, grad_gain_attn, grad_gain_ffn = results["small"]
    return (
        looked_up,
        grad_pieces,
        grad_script,
        grad_gain_attn.reshape(width),
        grad_gain_ffn.reshape(width),
        grad_w_qkv,
        grad_w_out,
        grad_w_up,
        grad_w_down,
        grad_w_proj,
    )


def solution(mesh):
    in_specs = (
        P(("ent", "rep"), None, None),
        P(("ent", "rep")),
        P(("ent", "rep")),
        P(),
        P(),
        P(),
        P(),
        P(),
        P(),
        P(),
        P(None, "ent"),
        P("rep", None),
        P("ent", "rep", None),
    )
    out_specs = (
        P("ent", "rep", None),
        P(("ent", "rep"), None, None),
        P(),
        P(),
        P(),
        P(),
        P(),
        P(),
        P(),
        P(None, "ent"),
    )
    return jax.shard_map(
        per_device, mesh=mesh, in_specs=in_specs, out_specs=out_specs, check_vma=False
    )
```

profile of v0, /device:TPU:0, one launch (start us, length us, event | category | flops | bytes accessed | tf_op | source)
XLA Modules:
  0.0 207.2 jit_solution(3297285890410170912)
XLA Ops:
  0.6 1.0 fusion.2.refs_0_
  1.7 2.2 %copy-done = bf16[256,4,2048]{2,1,0:T(4,128)(2,1)S(1)} copy-done((bf16[256,4,2048]{2,1,0:T(4,128)(2,1)S(1)}, bf16[256,4,2048]{2,1,0:T(4,128)(2,1)}, u32[]{:S(2)}) %copy-start) | copy-done | bytes 4194328
  3.9 0.9 copy-done.9
  4.8 11.5 %scatter_rows.2 = (bf16[2048,256]{1,0:T(8,128)(2,1)}, bf16[2048,512]{1,0:T(8,128)(2,1)}, f32[8,128]{1,0:T(8,128)S(1)}) custom-call(s32[4,2048]{1,0:T(4,128)S(1)} %fusion.2.refs_0_, bf16[256,4,2048]{2,1,0:T(4,128)(2,1)S(1)} %copy-done, bf16[512,256]{1,0:T(8,128)(2,1)S(1)} %copy-done.9), custom_call_target="tpu_custom_call" | custom-call | flops 41999998976 | bytes 126000000 | tf_op jit(solution)/shard_map/scatter_rows/pallas_call | solution.py:66
  17.5 2.2 %copy-done.1 = bf16[256,4,2048]{2,1,0:T(4,128)(2,1)S(1)} copy-done((bf16[256,4,2048]{2,1,0:T(4,128)(2,1)S(1)}, bf16[256,4,2048]{2,1,0:T(4,128)(2,1)}, u32[]{:S(2)}) %copy-start.1) | copy-done | bytes 4194328
  19.7 11.0 %scatter_rows.3 = (bf16[2048,256]{1,0:T(8,128)(2,1)}, f32[2048,512]{1,0:T(8,128)S(1)}, f32[8,128]{1,0:T(8,128)S(1)}) custom-call(s32[4,2048]{1,0:T(4,128)S(1)} %fusion.2.refs_0_, bf16[256,4,2048]{2,1,0:T(4,128)(2,1)S(1)} %copy-done.1, bf16[512,256]{1,0:T(8,128)(2,1)S(1)} %copy-done.10, f32[8,128]{1,0:T(8,128)S(1)} %get-tuple-element.148.refs_3_), custom_call_target="tpu_custom_call" | custom-call | flops 41999998976 | bytes 126000000 | tf_op jit(solution)/shard_map/scatter_rows/pallas_call | solution.py:66
  31.2 2.6 %collective-permute-start.1 = (bf16[2,4,128,256]{3,2,1,0:T(8,128)(2,1)S(1)}, bf16[2,4,128,256]{3,2,1,0:T(8,128)(2,1)S(1)}, u32[]{:S(2)}, u32[]{:S(2)}) collective-permute-start(bf16[2,4,128,256]{3,2,1,0:T(8,128)(2,1)S(1)} %get-tuple-element.156), channel_id=1, source_target_pairs={{0,2},{2,0},{4,6},{6,4},{8,10},{10,8},{12,14},{14,12},{16,18},{18,... | collective-permute-start | bytes 1572872 | tf_op jit(solution)/shard_map/ppermute | solution.py:94
  33.8 1.5 collective-permute-start.2
  35.3 11.2 %attn_forward.1 = (bf16[1024,512]{1,0:T(8,128)(2,1)S(1)}, bf16[1024,1536]{1,0:T(8,128)(2,1)}, bf16[1024,512]{1,0:T(8,128)(2,1)S(1)}, f32[1024,512]{1,0:T(8,128)S...) custom-call(bf16[128,8,512]{2,1,0:T(8,128)(2,1)S(1)} %copy-done.6, ...), custom_call_target="tpu_custom_call" | custom-call | flops 35999997952 | bytes 108000000 | tf_op jit(solution)/shard_map/attn_forward/pallas_call | solution.py:66
  46.6 1.2 collective-permute-done.2.refs_3_
  48.0 1.6 collective-permute-start.3
  50.2 8.0 %ffn_forward.2 = (f32[1024,1024]{1,0:T(8,128)}, bf16[128,1024]{1,0:T(8,128)(2,1)S(1)}, f32[128,512]{1,0:T(8,128)S(1)}, f32[8,128]{1,0:T(8,128)S(1)}) custom-call(s32[1024,1]{1,0:T(8,128)S(1)} %broadcast_in_dim_reshape.8.refs_2_.refs_0_.refs_1_, s32[128,1]{1,0:T(8,128)S(1)} %copy.32.refs_1_, f32[1024,512]{1,0:T(8,128)S(1)} %get-tuple-element.153.refs_2_.refs_4_, ...), custom_call_target="tpu_custom_call" | custom-call | flops 20999999488 | bytes 63000000 | tf_op jit(solution)/shard_map/ffn_forward/pallas_call | solution.py:66
  58.3 1.7 collective-permute-start.5
  59.9 2.6 %collective-permute-start.6 = (bf16[128,512]{1,0:T(8,128)(2,1)S(1)}, bf16[128,512]{1,0:T(8,128)(2,1)S(1)}, u32[]{:S(2)}, u32[]{:S(2)}) collective-permute-start(bf16[128,512]{1,0:T(8,128)(2,1)S(1)} %get-tuple-element.171), channel_id=1, source_target_pairs={{0,16},{2,18},{4,20},{6,22},{8,24},{10,26},{12,28},{14,30},{16,0},... | collective-permute-start | bytes 393224 | tf_op jit(solution)/shard_map/ppermute | solution.py:94
  62.7 8.0 %ffn_forward.3 = (f32[1024,1024]{1,0:T(8,128)}, bf16[128,1024]{1,0:T(8,128)(2,1)S(1)}, bf16[128,512]{1,0:T(8,128)(2,1)S(1)}, f32[8,128]{1,0:T(8,128)S(1)}) custom-call(s32[1024,1]{1,0:T(8,128)S(1)} %broadcast_in_dim_reshape.8.refs_2_.refs_0_.refs_1_, s32[128,1]{1,0:T(8,128)S(1)} %copy.32.refs_1_, f32[128,512]{1,0:T(8,128)S(1)} %get-tuple-element.161.refs_2_, ...), custom_call_target="tpu_custom_call" | custom-call | flops 20999999488 | bytes 63000000 | tf_op jit(solution)/shard_map/ffn_forward/pallas_call | solution.py:66
  70.7 1.6 collective-permute-done.6.refs_2_
  72.4 2.5 %collective-permute-start.10 = (bf16[128,512]{1,0:T(8,128)(2,1)S(1)}, bf16[128,512]{1,0:T(8,128)(2,1)S(1)}, u32[]{:S(2)}, u32[]{:S(2)}) collective-permute-start(bf16[128,512]{1,0:T(8,128)(2,1)S(1)} %get-tuple-element.175.refs_0_), channel_id=1, source_target_pairs={{0,24},{2,26},{4,28},{6,30},{8,16},{10,18},{12,20},{14,22},{16,8},... | collective-permute-start | bytes 393224 | tf_op jit(solution)/shard_map/ppermute | solution.py:94
  74.9 1.1 collective-permute-start.8
  76.9 2.5 %tall_weight.1 = (f32[16,64,512]{2,1,0:T(8,128)S(1)}, bf16[16,64,512]{2,1,0:T(8,128)(2,1)S(1)}, f32[8,128]{1,0:T(8,128)S(1)}) custom-call(s32[32]{0:T(128)S(1)} %iota_xor_fusion.refs_0_, bf16[128,1024]{1,0:T(8,128)(2,1)S(1)} %get-tuple-element.179.refs_1_, bf16[128,1024]{1,0:T(8,128)(2,1)S(1)} %get-tuple-element.180.refs_2_, ...), custom_call_target="tpu_custom_call" | custom-call | flops 8999999488 | bytes 27000000 | tf_op jit(solution)/shard_map/tall_weight/pallas_call | solution.py:66
  80.3 6.8 %ffn_back.1 = (bf16[1024,2048]{1,0:T(8,128)(2,1)S(1)}, f32[1024,512]{1,0:T(8,128)S(1)}, bf16[1024,512]{1,0:T(8,128)(2,1)S(1)}, f32[1,512]{1,0:T(1,128)S(1)}, f32[8,128]{1,0:T(8,128)S(1)}) custom-call(f32[128,512]{1,0:T(8,128)S(1)} %get-tuple-element.176.refs_0_, s32[1024,1]{1,0:T(8,128)S(1)} %broadcast_in_dim_reshape.8.refs_2_.refs_0_.refs_1_, ...), custom_call_target="tpu_custom_call" | custom-call | flops 44999999488 | bytes 135000000 | tf_op jit(solution)/shard_map/ffn_back/pallas_call | solution.py:66
  87.2 1.6 collective-permute-start.11
  89.4 4.4 %wide_weight.1 = (f32[16,64,512]{2,1,0:T(8,128)S(1)}, bf16[16,64,512]{2,1,0:T(8,128)(2,1)S(1)}, f32[8,128]{1,0:T(8,128)S(1)}) custom-call(s32[32]{0:T(128)S(1)} %iota_xor_fusion.refs_0_, bf16[1024,512]{1,0:T(8,128)(2,1)S(1)} %get-tuple-element.154.refs_3_.refs_1_, bf16[1024,2048]{1,0:T(8,128)(2,1)S(1)} %get-tuple-element.186.refs_2_, ...), custom_call_target="tpu_custom_call" | custom-call | flops 24000000000 | bytes 72000000 | tf_op jit(solution)/shard_map/wide_weight/pallas_call | solution.py:66
  93.9 1.2 collective-permute-done.11.refs_1_
  95.1 1.3 collective-permute-done.12.refs_3_
  97.1 1.0 collective-permute-start.14
  98.3 6.3 %heads_back.1 = (bf16[1024,1536]{1,0:T(8,128)(2,1)S(1)}, f32[8,128]{1,0:T(8,128)S(1)}) custom-call(s32[1024,1]{1,0:T(8,128)S(1)} %broadcast_in_dim_reshape.8.refs_2_.refs_0_.refs_1_, bf16[512,512]{1,0:T(8,128)(2,1)S(1)} %copy-done.8, bf16[1024,1536]{1,0:T(8,128)(2,1)S(1)} %copy-done.20, bf16[1024,512]{1,0:T(8,128)(2,1)S(1)} %get-tuple-element.193.refs_3_.refs_4_, ...), custom_call_target="tpu_custom_call" | custom-call | flops 38999998464 | bytes 117000000 | tf_op jit(solution)/shard_map/heads_back/pallas_call | solution.py:66
  105.8 1.5 collective-permute-start.20
  107.3 4.3 %two_weights.1 = (f32[16,64,512]{2,1,0:T(8,128)S(1)}, bf16[16,64,512]{2,1,0:T(8,128)(2,1)S(1)}, f32[8,128]{1,0:T(8,128)S(1)}) custom-call(s32[32]{0:T(128)S(1)} %iota_xor_fusion.refs_0_, bf16[1024,512]{1,0:T(8,128)(2,1)S(1)} %get-tuple-element.191.refs_1_, bf16[1024,1536]{1,0:T(8,128)(2,1)S(1)} %get-tuple-element.195.refs_2_.refs_5_, ...), custom_call_target="tpu_custom_call" | custom-call | flops 15000000512 | bytes 45000000 | tf_op jit(solution)/shard_map/two_weights/pallas_call | solution.py:66
  112.4 1.0 copy-done.5
  113.7 6.8 %attn_back.1 = (f32[128,8,512]{2,1,0:T(8,128)}, f32[32,512]{1,0:T(8,128)S(1)}, f32[8,128]{1,0:T(8,128)S(1)}) custom-call(bf16[128,8,512]{2,1,0:T(8,128)(2,1)S(1)} %copy-done.7, s32[1024,1]{1,0:T(8,128)S(1)} %broadcast_in_dim_reshape.9.refs_1_, f32[16,512]{1,0:T(8,128)S(1)} %copy-done.12, f32[1,512]{1,0:T(1,128)S(1)} %bitcast.38, ...), custom_call_target="tpu_custom_call" | custom-call | flops 27000000512 | bytes 81000000 | tf_op jit(solution)/shard_map/attn_back/pallas_call | solution.py:66
  121.6 1.1 collective-permute-start.22
  122.9 1.0 collective-permute-start.26
  123.9 1.5 collective-permute-start.27
  125.4 3.3 %table_and_grad.1 = (bf16[256,4096]{1,0:T(8,128)(2,1)S(1)}, f32[512,256]{1,0:T(8,128)S(1)}, f32[8,128]{1,0:T(8,128)S(1)}) custom-call(bf16[2048,512]{1,0:T(8,128)(2,1)S(1)} %bitcast.24, bf16[2048,512]{1,0:T(8,128)(2,1)S(1)} %bitcast.25, bf16[512,256]{1,0:T(8,128)(2,1)S(1)} %copy-done.10, bf16[2048,256]{1,0:T(8,128)(2,1)S(1)} %copy-done.19, ...), custom_call_target="tpu_custom_call" | custom-call | flops 15000000512 | bytes 45000000 | tf_op jit(solution)/shard_map/table_and_grad/pallas_call | solution.py:66
  128.7 1.6 collective-permute-done.21.refs_1_
  131.0 1.1 collective-permute-start.23
  132.1 2.0 collective-permute-start.24
  134.1 1.4 collective-permute-start.25
  135.4 8.2 %lookup.3 = (bf16[256,4,2048]{2,1,0:T(4,128)(2,1)}, f32[8,128]{1,0:T(8,128)S(1)}) custom-call(s32[4,2048]{1,0:T(4,128)S(1)} %fusion.2.refs_0_, bf16[256,4096]{1,0:T(8,128)(2,1)S(1)} %get-tuple-element.219.refs_1_, f32[8,128]{1,0:T(8,128)S(1)} %get-tuple-element.234.refs_2_), custom_call_target="tpu_custom_call" | custom-call | flops 27000000512 | bytes 81000000 | tf_op jit(solution)/shard_map/lookup/pallas_call | solution.py:66
  143.7 1.5 collective-permute-start.31
  145.3 1.1 collective-permute-start.32
  146.4 1.1 collective-permute-start.28
  147.5 2.0 collective-permute-start.29
  149.5 1.4 collective-permute-start.30
  150.9 8.2 %lookup.4 = (bf16[256,4,2048]{2,1,0:T(4,128)(2,1)}, f32[8,128]{1,0:T(8,128)S(1)}) custom-call(s32[4,2048]{1,0:T(4,128)S(1)} %fusion.2.refs_0_, bf16[256,4096]{1,0:T(8,128)(2,1)S(1)} %get-tuple-element.219.refs_1_, f32[8,128]{1,0:T(8,128)S(1)} %get-tuple-element.243.refs_2_, ...), custom_call_target="tpu_custom_call", output_to_operand_aliasing={{0}: (3, {})} | custom-call | flops 27000000512 | bytes 81000000 | tf_op jit(solution)/shard_map/lookup/pallas_call | solution.py:66
  159.3 2.9 %collective-permute-start.36 = (bf16[64,512]{1,0:T(8,128)(2,1)S(1)}, bf16[64,512]{1,0:T(8,128)(2,1)S(1)}, u32[]{:S(2)}, u32[]{:S(2)}) collective-permute-start(bf16[64,512]{1,0:T(8,128)(2,1)S(1)} %get-tuple-element.255), channel_id=1, source_target_pairs={{0,16},{2,18},{4,20},{6,22},{8,24},{10,26},{12,28},{14,30},{16,0},... | collective-permute-start | bytes 196616 | tf_op jit(solution)/shard_map/ppermute | solution.py:94
  162.2 1.4 collective-permute-start.37
  163.6 1.0 collective-permute-start.34
  165.2 5.7 %lookup.5 = (bf16[256,4,2048]{2,1,0:T(4,128)(2,1)}, f32[8,128]{1,0:T(8,128)S(1)}) custom-call(s32[4,2048]{1,0:T(4,128)S(1)} %fusion.2.refs_0_, bf16[256,4096]{1,0:T(8,128)(2,1)S(1)} %get-tuple-element.219.refs_1_, f32[8,128]{1,0:T(8,128)S(1)} %get-tuple-element.247.refs_2_, ...), custom_call_target="tpu_custom_call", output_to_operand_aliasing={{0}: (3, {})} | custom-call | flops 17999998976 | bytes 54000000 | tf_op jit(solution)/shard_map/lookup/pallas_call | solution.py:66
  171.1 1.5 collective-permute-start.39
  172.6 1.1 collective-permute-start.38
  173.7 3.0 %collective-permute-start.41 = (bf16[64,512]{1,0:T(8,128)(2,1)S(1)}, bf16[64,512]{1,0:T(8,128)(2,1)S(1)}, u32[]{:S(2)}, u32[]{:S(2)}) collective-permute-start(bf16[64,512]{1,0:T(8,128)(2,1)S(1)} %get-tuple-element.261.refs_0_), channel_id=1, source_target_pairs={{0,16},{2,18},{4,20},{6,22},{8,24},{10,26},{12,28},{14,30},{16,0},... | collective-permute-start | bytes 196616 | tf_op jit(solution)/shard_map/ppermute | solution.py:94
  176.9 2.5 %collective-permute-start.42 = (bf16[64,512]{1,0:T(8,128)(2,1)S(1)}, bf16[64,512]{1,0:T(8,128)(2,1)S(1)}, u32[]{:S(2)}, u32[]{:S(2)}) collective-permute-start(bf16[64,512]{1,0:T(8,128)(2,1)S(1)} %get-tuple-element.261.refs_0_), channel_id=1, source_target_pairs={{0,24},{2,26},{4,28},{6,30},{8,16},{10,18},{12,20},{14,22},{16,8},... | collective-permute-start | bytes 196616 | tf_op jit(solution)/shard_map/ppermute | solution.py:94
  179.3 2.3 %collective-permute-done.41.refs_2_ = bf16[64,512]{1,0:T(8,128)(2,1)S(1)} collective-permute-done((bf16[64,512]{1,0:T(8,128)(2,1)S(1)}, bf16[64,512]{1,0:T(8,128)(2,1)S(1)}, u32[]{:S(2)}, u32[]{:S(2)}) %collective-permute-start.41) | collective-permute-done | bytes 65568 | tf_op jit(solution)/shard_map/ppermute | solution.py:94
  181.6 1.5 collective-permute-done.42.refs_3_
  183.7 1.1 collective-permute-start.44
  184.8 0.8 exchange.42
  185.6 5.5 %collective-permute-done.43.refs_1_ = bf16[4,64,256]{2,1,0:T(8,128)(2,1)S(1)} collective-permute-done((bf16[4,64,256]{2,1,0:T(8,128)(2,1)S(1)}, bf16[4,64,256]{2,1,0:T(8,128)(2,1)S(1)}, u32[]{:S(2)}, u32[]{:S(2)}) %collective-permute-start.43) | collective-permute-done | bytes 131104 | tf_op jit(solution)/shard_map/ppermute | solution.py:94
  191.4 1.1 collective-permute-start.48
  192.5 1.5 collective-permute-start.49
  194.0 3.2 %unpack.2 = (f32[2048,512]{1,0:T(8,128)}, f32[8,128]{1,0:T(8,128)S(1)}) custom-call(s32[32]{0:T(128)S(1)} %iota_xor_fusion.refs_0_, bf16[16,64,512]{2,1,0:T(8,128)(2,1)S(1)} %bitcast.31, bf16[16,64,512]{2,1,0:T(8,128)(2,1)S(1)} %bitcast.32, f32[8,128]{1,0:T(8,128)S(1)} %get-tuple-element.271.refs_3_), custom_call_target="tpu_custom_call" | custom-call | flops 15000000512 | bytes 45000000 | tf_op jit(solution)/shard_map/unpack/pallas_call | solution.py:66
  197.2 3.2 %unpack.3 = (f32[512,2048]{1,0:T(8,128)}, f32[16,512]{1,0:T(8,128)}, f32[1,512]{1,0:T(1,128)}, f32[1,512]{1,0:T(1,128)}, f32[8,128]{1,0:T(8,128)S(1)}) custom-call(s32[32]{0:T(128)S(1)} %iota_xor_fusion.refs_0_, bf16[16,80,512]{2,1,0:T(8,128)(2,1)S(1)} %bitcast.26, bf16[16,80,512]{2,1,0:T(8,128)(2,1)S(1)} %bitcast.27, f32[8,128]{1,0:T(8,128)S(1)} %get-tuple-element.272.refs_3_), custom_call_target="tpu_custom_call" | custom-call | flops 15000000512 | bytes 45000000 | tf_op jit(solution)/shard_map/unpack/pallas_call | solution.py:66
  201.1 2.6 %collective-permute-done.50 = bf16[2,2,4,64,512]{4,3,2,1,0:T(8,128)(2,1)S(1)} collective-permute-done((bf16[2,2,4,64,512]{4,3,2,1,0:T(8,128)(2,1)S(1)}, bf16[2,2,4,64,512]{4,3,2,1,0:T(8,128)(2,1)S(1)}, u32[]{:S(2)}, u32[]{:S(2)}) %collective-permute-start.50) | collective-permute-done | bytes 1048608 | tf_op jit(solution)/shard_map/ppermute | solution.py:94
  203.7 3.5 %unpack_two.1 = (f32[512,1536]{1,0:T(8,128)}, f32[512,512]{1,0:T(8,128)}, f32[8,128]{1,0:T(8,128)}) custom-call(s32[32]{0:T(128)S(1)} %iota_xor_fusion.refs_0_, bf16[16,64,512]{2,1,0:T(8,128)(2,1)S(1)} %bitcast.33, bf16[16,64,512]{2,1,0:T(8,128)(2,1)S(1)} %bitcast.34, f32[8,128]{1,0:T(8,128)S(1)} %get-tuple-element.280.refs_3_), custom_call_target="tpu_custom_call" | custom-call | flops 15000000512 | bytes 45000000 | tf_op jit(solution)/shard_map/unpack_two/pallas_call | solution.py:66
  (133 shorter events, 13.7 us)
Async XLA Ops:
  4.8 11.9 %copy-start.21 = (s32[128]{0:T(128)S(1)}, s32[128]{0:T(128)}, u32[]{:S(2)}) copy-start(s32[128]{0:T(128)} %param.14) | copy-start | bytes 1540
  4.8 12.2 %copy-start.22 = (s32[128]{0:T(128)S(1)}, s32[128]{0:T(128)}, u32[]{:S(2)}) copy-start(s32[128]{0:T(128)} %param.15) | copy-start | bytes 1540
  4.8 12.6 %copy-start.10 = (bf16[512,256]{1,0:T(8,128)(2,1)S(1)}, bf16[512,256]{1,0:T(8,128)(2,1)}, u32[]{:S(2)}) copy-start(bf16[512,256]{1,0:T(8,128)(2,1)} %refs_2_.7) | copy-start | bytes 786436
  16.3 14.4 %collective-permute-start = (bf16[2,2,4,128,512]{4,3,2,1,0:T(8,128)(2,1)}, bf16[2,2,4,128,512]{4,3,2,1,0:T(8,128)(2,1)S(1)}, u32[]{:S(2)}, u32[]{:S(2)}) collective-permute-start(bf16[2,2,4,128,512]{4,3,2,1,0:T(8,128)(2,1)} %bitcast.4), channel_id=1, source_target_pairs={{0,1},{1,0},{2,3},{3,2},{4,5},{5,4},{6,7},{7,6},{8,9},{9,8},{10,11... | collective-permute-start | bytes 6291464 | tf_op jit(solution)/shard_map/ppermute | solution.py:94
  30.7 4.6 %copy-start.4 = (bf16[512,1536]{1,0:T(8,128)(2,1)S(1)}, bf16[512,1536]{1,0:T(8,128)(2,1)}, u32[]{:S(2)}) copy-start(bf16[512,1536]{1,0:T(8,128)(2,1)} %refs_4_.5) | copy-start | bytes 4718596
  30.7 4.6 %copy-start.6 = (bf16[128,8,512]{2,1,0:T(8,128)(2,1)S(1)}, bf16[128,8,512]{2,1,0:T(8,128)(2,1)}, u32[]{:S(2)}) copy-start(bf16[128,8,512]{2,1,0:T(8,128)(2,1)} %refs_0_.3) | copy-start | bytes 3145732
  30.7 4.6 %copy-start.8 = (bf16[512,512]{1,0:T(8,128)(2,1)S(1)}, bf16[512,512]{1,0:T(8,128)(2,1)}, u32[]{:S(2)}) copy-start(bf16[512,512]{1,0:T(8,128)(2,1)} %refs_1_.5) | copy-start | bytes 1572868
  30.7 4.6 %copy-start.11 = (f32[16,512]{1,0:T(8,128)S(1)}, f32[16,512]{1,0:T(8,128)}, u32[]{:S(2)}) copy-start(f32[16,512]{1,0:T(8,128)} %refs_2_.6) | copy-start | bytes 98308
  30.7 4.6 %copy-start.13 = (f32[512]{0:T(512)S(1)}, f32[512]{0:T(512)}, u32[]{:S(2)}) copy-start(f32[512]{0:T(512)} %param.18) | copy-start | bytes 6148
  30.7 4.6 %copy-start.14 = (f32[512]{0:T(512)S(1)}, f32[512]{0:T(512)}, u32[]{:S(2)}) copy-start(f32[512]{0:T(512)} %param.17) | copy-start | bytes 6148
  31.2 15.4 %collective-permute-start.1 = (bf16[2,4,128,256]{3,2,1,0:T(8,128)(2,1)S(1)}, bf16[2,4,128,256]{3,2,1,0:T(8,128)(2,1)S(1)}, u32[]{:S(2)}, u32[]{:S(2)}) collective-permute-start(bf16[2,4,128,256]{3,2,1,0:T(8,128)(2,1)S(1)} %get-tuple-element.156), channel_id=1, source_target_pairs={{0,2},{2,0},{4,6},{6,4},{8,10},{10,8},{12,14},{14,12},{16,18},{18,... | collective-permute-start | bytes 1572872 | tf_op jit(solution)/shard_map/ppermute | solution.py:94
  33.8 14.1 %collective-permute-start.2 = (bf16[2,4,128,256]{3,2,1,0:T(8,128)(2,1)S(1)}, bf16[2,4,128,256]{3,2,1,0:T(8,128)(2,1)S(1)}, u32[]{:S(2)}, u32[]{:S(2)}) collective-permute-start(bf16[2,4,128,256]{3,2,1,0:T(8,128)(2,1)S(1)} %get-tuple-element.158), channel_id=1, source_target_pairs={{0,4},{2,6},{4,0},{6,2},{8,12},{10,14},{12,8},{14,10},{16,20},{18,... | collective-permute-start | bytes 1572872 | tf_op jit(solution)/shard_map/ppermute | solution.py:94
  48.0 10.1 %collective-permute-start.3 = (bf16[4,128,256]{2,1,0:T(8,128)(2,1)S(1)}, bf16[4,128,256]{2,1,0:T(8,128)(2,1)S(1)}, u32[]{:S(2)}, u32[]{:S(2)}) collective-permute-start(bf16[4,128,256]{2,1,0:T(8,128)(2,1)S(1)} %get-tuple-element.163), channel_id=1, source_target_pairs={{0,4},{2,6},{4,0},{6,2},{8,12},{10,14},{12,8},{14,10},{16,20},{18,... | collective-permute-start | bytes 786440 | tf_op jit(solution)/shard_map/ppermute | solution.py:94
  49.6 8.5 %collective-permute-start.4 = (bf16[4,128,256]{2,1,0:T(8,128)(2,1)S(1)}, bf16[4,128,256]{2,1,0:T(8,128)(2,1)S(1)}, u32[]{:S(2)}, u32[]{:S(2)}) collective-permute-start(bf16[4,128,256]{2,1,0:T(8,128)(2,1)S(1)} %get-tuple-element.165), channel_id=1, source_target_pairs={{0,2},{2,0},{4,6},{6,4},{8,10},{10,8},{12,14},{14,12},{16,18},{18,... | collective-permute-start | bytes 786440 | tf_op jit(solution)/shard_map/ppermute | solution.py:94
  58.3 12.4 %collective-permute-start.5 = (bf16[128,512]{1,0:T(8,128)(2,1)S(1)}, bf16[128,512]{1,0:T(8,128)(2,1)S(1)}, u32[]{:S(2)}, u32[]{:S(2)}) collective-permute-start(bf16[128,512]{1,0:T(8,128)(2,1)S(1)} %get-tuple-element.170), channel_id=1, source_target_pairs={{0,8},{2,10},{4,12},{6,14},{8,0},{10,2},{12,4},{14,6},{16,24},{18,... | collective-permute-start | bytes 393224 | tf_op jit(solution)/shard_map/ppermute | solution.py:94
  59.9 12.4 %collective-permute-start.6 = (bf16[128,512]{1,0:T(8,128)(2,1)S(1)}, bf16[128,512]{1,0:T(8,128)(2,1)S(1)}, u32[]{:S(2)}, u32[]{:S(2)}) collective-permute-start(bf16[128,512]{1,0:T(8,128)(2,1)S(1)} %get-tuple-element.171), channel_id=1, source_target_pairs={{0,16},{2,18},{4,20},{6,22},{8,24},{10,26},{12,28},{14,30},{16,0},... | collective-permute-start | bytes 393224 | tf_op jit(solution)/shard_map/ppermute | solution.py:94
  62.5 9.8 %collective-permute-start.7 = (bf16[128,512]{1,0:T(8,128)(2,1)S(1)}, bf16[128,512]{1,0:T(8,128)(2,1)S(1)}, u32[]{:S(2)}, u32[]{:S(2)}) collective-permute-start(bf16[128,512]{1,0:T(8,128)(2,1)S(1)} %get-tuple-element.172), channel_id=1, source_target_pairs={{0,24},{2,26},{4,28},{6,30},{8,16},{10,18},{12,20},{14,22},{16,8},... | collective-permute-start | bytes 393224 | tf_op jit(solution)/shard_map/ppermute | solution.py:94
  72.4 14.8 %collective-permute-start.10 = (bf16[128,512]{1,0:T(8,128)(2,1)S(1)}, bf16[128,512]{1,0:T(8,128)(2,1)S(1)}, u32[]{:S(2)}, u32[]{:S(2)}) collective-permute-start(bf16[128,512]{1,0:T(8,128)(2,1)S(1)} %get-tuple-element.175.refs_0_), channel_id=1, source_target_pairs={{0,24},{2,26},{4,28},{6,30},{8,16},{10,18},{12,20},{14,22},{16,8},... | collective-permute-start | bytes 393224 | tf_op jit(solution)/shard_map/ppermute | solution.py:94
  74.9 12.2 %collective-permute-start.8 = (bf16[128,512]{1,0:T(8,128)(2,1)S(1)}, bf16[128,512]{1,0:T(8,128)(2,1)S(1)}, u32[]{:S(2)}, u32[]{:S(2)}) collective-permute-start(bf16[128,512]{1,0:T(8,128)(2,1)S(1)} %get-tuple-element.175.refs_0_), channel_id=1, source_target_pairs={{0,8},{2,10},{4,12},{6,14},{8,0},{10,2},{12,4},{14,6},{16,24},{18,... | collective-permute-start | bytes 393224 | tf_op jit(solution)/shard_map/ppermute | solution.py:94
  76.0 11.2 %collective-permute-start.9 = (bf16[128,512]{1,0:T(8,128)(2,1)S(1)}, bf16[128,512]{1,0:T(8,128)(2,1)S(1)}, u32[]{:S(2)}, u32[]{:S(2)}) collective-permute-start(bf16[128,512]{1,0:T(8,128)(2,1)S(1)} %get-tuple-element.175.refs_0_), channel_id=1, source_target_pairs={{0,16},{2,18},{4,20},{6,22},{8,24},{10,26},{12,28},{14,30},{16,0},... | collective-permute-start | bytes 393224 | tf_op jit(solution)/shard_map/ppermute | solution.py:94
  76.8 2.6 %copy-start.16 = (f32[1024,1024]{1,0:T(8,128)S(1)}, f32[1024,1024]{1,0:T(8,128)}, u32[]{:S(2)}) copy-start(f32[1024,1024]{1,0:T(8,128)} %get-tuple-element.177.refs_2_) | copy-start | bytes 12582916
  76.9 3.5 %copy-start.17 = (f32[1024,1024]{1,0:T(8,128)S(1)}, f32[1024,1024]{1,0:T(8,128)}, u32[]{:S(2)}) copy-start(f32[1024,1024]{1,0:T(8,128)} %get-tuple-element.178.refs_3_) | copy-start | bytes 12582916
  79.4 25.2 %collective-permute-start.15 = (bf16[2,2,4,64,512]{4,3,2,1,0:T(8,128)(2,1)S(1)}, bf16[2,2,4,64,512]{4,3,2,1,0:T(8,128)(2,1)S(1)}, u32[]{:S(2)}, u32[]{:S(2)}) collective-permute-start(bf16[2,2,4,64,512]{4,3,2,1,0:T(8,128)(2,1)S(1)} %bitcast.28), channel_id=1, source_target_pairs={{0,1},{1,0},{2,3},{3,2},{4,5},{5,4},{6,7},{7,6},{8,9},{9,8},{10,11... | collective-permute-start | bytes 3145736 | tf_op jit(solution)/shard_map/ppermute | solution.py:94
  87.2 7.9 %collective-permute-start.11 = (bf16[4,128,256]{2,1,0:T(8,128)(2,1)S(1)}, bf16[4,128,256]{2,1,0:T(8,128)(2,1)S(1)}, u32[]{:S(2)}, u32[]{:S(2)}) collective-permute-start(bf16[4,128,256]{2,1,0:T(8,128)(2,1)S(1)} %get-tuple-element.184.refs_0_), channel_id=1, source_target_pairs={{0,4},{2,6},{4,0},{6,2},{8,12},{10,14},{12,8},{14,10},{16,20},{18,... | collective-permute-start | bytes 786440 | tf_op jit(solution)/shard_map/ppermute | solution.py:94
  88.8 7.6 %collective-permute-start.12 = (bf16[4,128,256]{2,1,0:T(8,128)(2,1)S(1)}, bf16[4,128,256]{2,1,0:T(8,128)(2,1)S(1)}, u32[]{:S(2)}, u32[]{:S(2)}) collective-permute-start(bf16[4,128,256]{2,1,0:T(8,128)(2,1)S(1)} %get-tuple-element.185.refs_2_), channel_id=1, source_target_pairs={{0,2},{2,0},{4,6},{6,4},{8,10},{10,8},{12,14},{14,12},{16,18},{18,... | collective-permute-start | bytes 786440 | tf_op jit(solution)/shard_map/ppermute | solution.py:94
  93.8 10.7 %collective-permute-start.16 = (bf16[2,2,4,64,512]{4,3,2,1,0:T(8,128)(2,1)S(1)}, bf16[2,2,4,64,512]{4,3,2,1,0:T(8,128)(2,1)S(1)}, u32[]{:S(2)}, u32[]{:S(2)}) collective-permute-start(bf16[2,2,4,64,512]{4,3,2,1,0:T(8,128)(2,1)S(1)} %bitcast.30), channel_id=1, source_target_pairs={{0,1},{1,0},{2,3},{3,2},{4,5},{5,4},{6,7},{7,6},{8,9},{9,8},{10,11... | collective-permute-start | bytes 3145736 | tf_op jit(solution)/shard_map/ppermute | solution.py:94
  96.5 15.2 %collective-permute-start.13 = (bf16[2,4,128,256]{3,2,1,0:T(8,128)(2,1)S(1)}, bf16[2,4,128,256]{3,2,1,0:T(8,128)(2,1)S(1)}, u32[]{:S(2)}, u32[]{:S(2)}) collective-permute-start(bf16[2,4,128,256]{3,2,1,0:T(8,128)(2,1)S(1)} %get-tuple-element.189.refs_0_), channel_id=1, source_target_pairs={{0,2},{2,0},{4,6},{6,4},{8,10},{10,8},{12,14},{14,12},{16,18},{18,... | collective-permute-start | bytes 1572872 | tf_op jit(solution)/shard_map/ppermute | solution.py:94
  97.1 14.9 %collective-permute-start.14 = (bf16[2,4,128,256]{3,2,1,0:T(8,128)(2,1)S(1)}, bf16[2,4,128,256]{3,2,1,0:T(8,128)(2,1)S(1)}, u32[]{:S(2)}, u32[]{:S(2)}) collective-permute-start(bf16[2,4,128,256]{3,2,1,0:T(8,128)(2,1)S(1)} %get-tuple-element.190.refs_2_), channel_id=1, source_target_pairs={{0,4},{2,6},{4,0},{6,2},{8,12},{10,14},{12,8},{14,10},{16,20},{18,... | collective-permute-start | bytes 1572872 | tf_op jit(solution)/shard_map/ppermute | solution.py:94
  104.9 15.6 %collective-permute-start.19 = (bf16[2,4,64,512]{3,2,1,0:T(8,128)(2,1)S(1)}, bf16[2,4,64,512]{3,2,1,0:T(8,128)(2,1)S(1)}, u32[]{:S(2)}, u32[]{:S(2)}) collective-permute-start(bf16[2,4,64,512]{3,2,1,0:T(8,128)(2,1)S(1)} %get-tuple-element.210), channel_id=1, source_target_pairs={{0,2},{2,0},{4,6},{6,4},{8,10},{10,8},{12,14},{14,12},{16,18},{18,... | collective-permute-start | bytes 1572872 | tf_op jit(solution)/shard_map/ppermute | solution.py:94
  105.8 15.0 %collective-permute-start.20 = (bf16[2,4,64,512]{3,2,1,0:T(8,128)(2,1)S(1)}, bf16[2,4,64,512]{3,2,1,0:T(8,128)(2,1)S(1)}, u32[]{:S(2)}, u32[]{:S(2)}) collective-permute-start(bf16[2,4,64,512]{3,2,1,0:T(8,128)(2,1)S(1)} %get-tuple-element.212), channel_id=1, source_target_pairs={{0,4},{2,6},{4,0},{6,2},{8,12},{10,14},{12,8},{14,10},{16,20},{18,... | collective-permute-start | bytes 1572872 | tf_op jit(solution)/shard_map/ppermute | solution.py:94
  111.6 11.1 %collective-permute-start.18 = (bf16[2,2,4,64,512]{4,3,2,1,0:T(8,128)(2,1)S(1)}, bf16[2,2,4,64,512]{4,3,2,1,0:T(8,128)(2,1)S(1)}, u32[]{:S(2)}, u32[]{:S(2)}) collective-permute-start(bf16[2,2,4,64,512]{4,3,2,1,0:T(8,128)(2,1)S(1)} %bitcast.29), channel_id=1, source_target_pairs={{0,1},{1,0},{2,3},{3,2},{4,5},{5,4},{6,7},{7,6},{8,9},{9,8},{10,11... | collective-permute-start | bytes 3145736 | tf_op jit(solution)/shard_map/ppermute | solution.py:94
  112.2 13.3 %collective-permute-start.17 = (bf16[2,2,4,128,512]{4,3,2,1,0:T(8,128)(2,1)S(1)}, bf16[2,2,4,128,512]{4,3,2,1,0:T(8,128)(2,1)S(1)}, u32[]{:S(2)}, u32[]{:S(2)}) collective-permute-start(bf16[2,2,4,128,512]{4,3,2,1,0:T(8,128)(2,1)S(1)} %get-tuple-element.204), channel_id=1, source_target_pairs={{0,1},{1,0},{2,3},{3,2},{4,5},{5,4},{6,7},{7,6},{8,9},{9,8},{10,11... | collective-permute-start | bytes 6291464 | tf_op jit(solution)/shard_map/ppermute | solution.py:94
  121.0 9.2 %collective-permute-start.21 = (bf16[4,64,512]{2,1,0:T(8,128)(2,1)S(1)}, bf16[4,64,512]{2,1,0:T(8,128)(2,1)S(1)}, u32[]{:S(2)}, u32[]{:S(2)}) collective-permute-start(bf16[4,64,512]{2,1,0:T(8,128)(2,1)S(1)} %get-tuple-element.221), channel_id=1, source_target_pairs={{0,4},{2,6},{4,0},{6,2},{8,12},{10,14},{12,8},{14,10},{16,20},{18,... | collective-permute-start | bytes 786440 | tf_op jit(solution)/shard_map/ppermute | solution.py:94
  121.6 9.2 %collective-permute-start.22 = (bf16[4,64,512]{2,1,0:T(8,128)(2,1)S(1)}, bf16[4,64,512]{2,1,0:T(8,128)(2,1)S(1)}, u32[]{:S(2)}, u32[]{:S(2)}) collective-permute-start(bf16[4,64,512]{2,1,0:T(8,128)(2,1)S(1)} %get-tuple-element.223), channel_id=1, source_target_pairs={{0,2},{2,0},{4,6},{6,4},{8,10},{10,8},{12,14},{14,12},{16,18},{18,... | collective-permute-start | bytes 786440 | tf_op jit(solution)/shard_map/ppermute | solution.py:94
  122.7 2.7 %copy-start.18 = (bf16[2048,256]{1,0:T(8,128)(2,1)S(1)}, bf16[2048,256]{1,0:T(8,128)(2,1)}, u32[]{:S(2)}) copy-start(bf16[2048,256]{1,0:T(8,128)(2,1)} %get-tuple-element.206.refs_4_) | copy-start | bytes 3145732
  122.7 2.7 %copy-start.19 = (bf16[2048,256]{1,0:T(8,128)(2,1)S(1)}, bf16[2048,256]{1,0:T(8,128)(2,1)}, u32[]{:S(2)}) copy-start(bf16[2048,256]{1,0:T(8,128)(2,1)} %get-tuple-element.205.refs_3_) | copy-start | bytes 3145732
  122.9 20.7 %collective-permute-start.26 = (bf16[2,4,64,256]{3,2,1,0:T(8,128)(2,1)S(1)}, bf16[2,4,64,256]{3,2,1,0:T(8,128)(2,1)S(1)}, u32[]{:S(2)}, u32[]{:S(2)}) collective-permute-start(bf16[2,4,64,256]{3,2,1,0:T(8,128)(2,1)S(1)} %get-tuple-element.231), channel_id=1, source_target_pairs={{0,2},{2,0},{4,6},{6,4},{8,10},{10,8},{12,14},{14,12},{16,18},{18,... | collective-permute-start | bytes 786440 | tf_op jit(solution)/shard_map/ppermute | solution.py:94
  123.9 19.7 %collective-permute-start.27 = (bf16[2,4,64,256]{3,2,1,0:T(8,128)(2,1)S(1)}, bf16[2,4,64,256]{3,2,1,0:T(8,128)(2,1)S(1)}, u32[]{:S(2)}, u32[]{:S(2)}) collective-permute-start(bf16[2,4,64,256]{3,2,1,0:T(8,128)(2,1)S(1)} %get-tuple-element.233), channel_id=1, source_target_pairs={{0,4},{2,6},{4,0},{6,2},{8,12},{10,14},{12,8},{14,10},{16,20},{18,... | collective-permute-start | bytes 786440 | tf_op jit(solution)/shard_map/ppermute | solution.py:94
  131.0 15.3 %collective-permute-start.23 = (bf16[160,512]{1,0:T(8,128)(2,1)S(1)}, bf16[160,512]{1,0:T(8,128)(2,1)S(1)}, u32[]{:S(2)}, u32[]{:S(2)}) collective-permute-start(bf16[160,512]{1,0:T(8,128)(2,1)S(1)} %get-tuple-element.227), channel_id=1, source_target_pairs={{0,8},{2,10},{4,12},{6,14},{8,0},{10,2},{12,4},{14,6},{16,24},{18,... | collective-permute-start | bytes 491528 | tf_op jit(solution)/shard_map/ppermute | solution.py:94
  132.1 14.2 %collective-permute-start.24 = (bf16[160,512]{1,0:T(8,128)(2,1)S(1)}, bf16[160,512]{1,0:T(8,128)(2,1)S(1)}, u32[]{:S(2)}, u32[]{:S(2)}) collective-permute-start(bf16[160,512]{1,0:T(8,128)(2,1)S(1)} %get-tuple-element.228), channel_id=1, source_target_pairs={{0,16},{2,18},{4,20},{6,22},{8,24},{10,26},{12,28},{14,30},{16,0},... | collective-permute-start | bytes 491528 | tf_op jit(solution)/shard_map/ppermute | solution.py:94
  134.1 12.2 %collective-permute-start.25 = (bf16[160,512]{1,0:T(8,128)(2,1)S(1)}, bf16[160,512]{1,0:T(8,128)(2,1)S(1)}, u32[]{:S(2)}, u32[]{:S(2)}) collective-permute-start(bf16[160,512]{1,0:T(8,128)(2,1)S(1)} %get-tuple-element.229), channel_id=1, source_target_pairs={{0,24},{2,26},{4,28},{6,30},{8,16},{10,18},{12,20},{14,22},{16,8},... | collective-permute-start | bytes 491528 | tf_op jit(solution)/shard_map/ppermute | solution.py:94
  143.7 15.3 %collective-permute-start.31 = (bf16[4,64,256]{2,1,0:T(8,128)(2,1)S(1)}, bf16[4,64,256]{2,1,0:T(8,128)(2,1)S(1)}, u32[]{:S(2)}, u32[]{:S(2)}) collective-permute-start(bf16[4,64,256]{2,1,0:T(8,128)(2,1)S(1)} %get-tuple-element.240), channel_id=1, source_target_pairs={{0,4},{2,6},{4,0},{6,2},{8,12},{10,14},{12,8},{14,10},{16,20},{18,... | collective-permute-start | bytes 393224 | tf_op jit(solution)/shard_map/ppermute | solution.py:94
  145.3 13.8 %collective-permute-start.32 = (bf16[4,64,256]{2,1,0:T(8,128)(2,1)S(1)}, bf16[4,64,256]{2,1,0:T(8,128)(2,1)S(1)}, u32[]{:S(2)}, u32[]{:S(2)}) collective-permute-start(bf16[4,64,256]{2,1,0:T(8,128)(2,1)S(1)} %get-tuple-element.242), channel_id=1, source_target_pairs={{0,2},{2,0},{4,6},{6,4},{8,10},{10,8},{12,14},{14,12},{16,18},{18,... | collective-permute-start | bytes 393224 | tf_op jit(solution)/shard_map/ppermute | solution.py:94
  146.4 15.8 %collective-permute-start.28 = (bf16[128,512]{1,0:T(8,128)(2,1)S(1)}, bf16[128,512]{1,0:T(8,128)(2,1)S(1)}, u32[]{:S(2)}, u32[]{:S(2)}) collective-permute-start(bf16[128,512]{1,0:T(8,128)(2,1)S(1)} %get-tuple-element.237.refs_0_), channel_id=1, source_target_pairs={{0,8},{2,10},{4,12},{6,14},{8,0},{10,2},{12,4},{14,6},{16,24},{18,... | collective-permute-start | bytes 393224 | tf_op jit(solution)/shard_map/ppermute | solution.py:94
  147.5 16.0 %collective-permute-start.29 = (bf16[128,512]{1,0:T(8,128)(2,1)S(1)}, bf16[128,512]{1,0:T(8,128)(2,1)S(1)}, u32[]{:S(2)}, u32[]{:S(2)}) collective-permute-start(bf16[128,512]{1,0:T(8,128)(2,1)S(1)} %get-tuple-element.237.refs_0_), channel_id=1, source_target_pairs={{0,16},{2,18},{4,20},{6,22},{8,24},{10,26},{12,28},{14,30},{16,0},... | collective-permute-start | bytes 393224 | tf_op jit(solution)/shard_map/ppermute | solution.py:94
  149.5 14.1 %collective-permute-start.30 = (bf16[128,512]{1,0:T(8,128)(2,1)S(1)}, bf16[128,512]{1,0:T(8,128)(2,1)S(1)}, u32[]{:S(2)}, u32[]{:S(2)}) collective-permute-start(bf16[128,512]{1,0:T(8,128)(2,1)S(1)} %get-tuple-element.237.refs_0_), channel_id=1, source_target_pairs={{0,24},{2,26},{4,28},{6,30},{8,16},{10,18},{12,20},{14,22},{16,8},... | collective-permute-start | bytes 393224 | tf_op jit(solution)/shard_map/ppermute | solution.py:94
  159.1 11.8 %collective-permute-start.35 = (bf16[64,512]{1,0:T(8,128)(2,1)S(1)}, bf16[64,512]{1,0:T(8,128)(2,1)S(1)}, u32[]{:S(2)}, u32[]{:S(2)}) collective-permute-start(bf16[64,512]{1,0:T(8,128)(2,1)S(1)} %get-tuple-element.254), channel_id=1, source_target_pairs={{0,8},{2,10},{4,12},{6,14},{8,0},{10,2},{12,4},{14,6},{16,24},{18,... | collective-permute-start | bytes 196616 | tf_op jit(solution)/shard_map/ppermute | solution.py:94
  159.3 11.6 %collective-permute-start.36 = (bf16[64,512]{1,0:T(8,128)(2,1)S(1)}, bf16[64,512]{1,0:T(8,128)(2,1)S(1)}, u32[]{:S(2)}, u32[]{:S(2)}) collective-permute-start(bf16[64,512]{1,0:T(8,128)(2,1)S(1)} %get-tuple-element.255), channel_id=1, source_target_pairs={{0,16},{2,18},{4,20},{6,22},{8,24},{10,26},{12,28},{14,30},{16,0},... | collective-permute-start | bytes 196616 | tf_op jit(solution)/shard_map/ppermute | solution.py:94
  162.2 8.7 %collective-permute-start.37 = (bf16[64,512]{1,0:T(8,128)(2,1)S(1)}, bf16[64,512]{1,0:T(8,128)(2,1)S(1)}, u32[]{:S(2)}, u32[]{:S(2)}) collective-permute-start(bf16[64,512]{1,0:T(8,128)(2,1)S(1)} %get-tuple-element.256), channel_id=1, source_target_pairs={{0,24},{2,26},{4,28},{6,30},{8,16},{10,18},{12,20},{14,22},{16,8},... | collective-permute-start | bytes 196616 | tf_op jit(solution)/shard_map/ppermute | solution.py:94
  163.6 7.4 %collective-permute-start.34 = (bf16[4,80,512]{2,1,0:T(8,128)(2,1)S(1)}, bf16[4,80,512]{2,1,0:T(8,128)(2,1)S(1)}, u32[]{:S(2)}, u32[]{:S(2)}) collective-permute-start(bf16[4,80,512]{2,1,0:T(8,128)(2,1)S(1)} %get-tuple-element.252.refs_2_), channel_id=1, source_target_pairs={{0,2},{2,0},{4,6},{6,4},{8,10},{10,8},{12,14},{14,12},{16,18},{18,... | collective-permute-start | bytes 983048 | tf_op jit(solution)/shard_map/ppermute | solution.py:94
  164.7 6.4 %collective-permute-start.33 = (bf16[4,64,512]{2,1,0:T(8,128)(2,1)S(1)}, bf16[4,64,512]{2,1,0:T(8,128)(2,1)S(1)}, u32[]{:S(2)}, u32[]{:S(2)}) collective-permute-start(bf16[4,64,512]{2,1,0:T(8,128)(2,1)S(1)} %get-tuple-element.251.refs_0_), channel_id=1, source_target_pairs={{0,4},{2,6},{4,0},{6,2},{8,12},{10,14},{12,8},{14,10},{16,20},{18,... | collective-permute-start | bytes 786440 | tf_op jit(solution)/shard_map/ppermute | solution.py:94
  170.9 13.9 %collective-permute-start.45 = (f32[512,256]{1,0:T(8,128)S(1)}, f32[512,256]{1,0:T(8,128)S(1)}, u32[]{:S(2)}, u32[]{:S(2)}) collective-permute-start(f32[512,256]{1,0:T(8,128)S(1)} %get-tuple-element.265.refs_0_), channel_id=1, source_target_pairs={{0,1},{1,0},{2,3},{3,2},{4,5},{5,4},{6,7},{7,6},{8,9},{9,8},{10,11... | collective-permute-start | bytes 1572872 | tf_op jit(solution)/shard_map/ppermute | solution.py:94
  171.1 20.0 %collective-permute-start.39 = (bf16[2,4,80,512]{3,2,1,0:T(8,128)(2,1)S(1)}, bf16[2,4,80,512]{3,2,1,0:T(8,128)(2,1)S(1)}, u32[]{:S(2)}, u32[]{:S(2)}) collective-permute-start(bf16[2,4,80,512]{3,2,1,0:T(8,128)(2,1)S(1)} %get-tuple-element.260.refs_2_), channel_id=1, source_target_pairs={{0,4},{2,6},{4,0},{6,2},{8,12},{10,14},{12,8},{14,10},{16,20},{18,... | collective-permute-start | bytes 1966088 | tf_op jit(solution)/shard_map/ppermute | solution.py:94
  172.6 4.3 %collective-permute-start.40 = (bf16[64,512]{1,0:T(8,128)(2,1)S(1)}, bf16[64,512]{1,0:T(8,128)(2,1)S(1)}, u32[]{:S(2)}, u32[]{:S(2)}) collective-permute-start(bf16[64,512]{1,0:T(8,128)(2,1)S(1)} %get-tuple-element.261.refs_0_), channel_id=1, source_target_pairs={{0,8},{2,10},{4,12},{6,14},{8,0},{10,2},{12,4},{14,6},{16,24},{18,... | collective-permute-start | bytes 196616 | tf_op jit(solution)/shard_map/ppermute | solution.py:94
  172.6 18.5 %collective-permute-start.38 = (bf16[2,4,64,512]{3,2,1,0:T(8,128)(2,1)S(1)}, bf16[2,4,64,512]{3,2,1,0:T(8,128)(2,1)S(1)}, u32[]{:S(2)}, u32[]{:S(2)}) collective-permute-start(bf16[2,4,64,512]{3,2,1,0:T(8,128)(2,1)S(1)} %get-tuple-element.259.refs_0_), channel_id=1, source_target_pairs={{0,2},{2,0},{4,6},{6,4},{8,10},{10,8},{12,14},{14,12},{16,18},{18,... | collective-permute-start | bytes 1572872 | tf_op jit(solution)/shard_map/ppermute | solution.py:94
  173.7 7.9 %collective-permute-start.41 = (bf16[64,512]{1,0:T(8,128)(2,1)S(1)}, bf16[64,512]{1,0:T(8,128)(2,1)S(1)}, u32[]{:S(2)}, u32[]{:S(2)}) collective-permute-start(bf16[64,512]{1,0:T(8,128)(2,1)S(1)} %get-tuple-element.261.refs_0_), channel_id=1, source_target_pairs={{0,16},{2,18},{4,20},{6,22},{8,24},{10,26},{12,28},{14,30},{16,0},... | collective-permute-start | bytes 196616 | tf_op jit(solution)/shard_map/ppermute | solution.py:94
  176.9 6.2 %collective-permute-start.42 = (bf16[64,512]{1,0:T(8,128)(2,1)S(1)}, bf16[64,512]{1,0:T(8,128)(2,1)S(1)}, u32[]{:S(2)}, u32[]{:S(2)}) collective-permute-start(bf16[64,512]{1,0:T(8,128)(2,1)S(1)} %get-tuple-element.261.refs_0_), channel_id=1, source_target_pairs={{0,24},{2,26},{4,28},{6,30},{8,16},{10,18},{12,20},{14,22},{16,8},... | collective-permute-start | bytes 196616 | tf_op jit(solution)/shard_map/ppermute | solution.py:94
  183.1 8.0 %collective-permute-start.43 = (bf16[4,64,256]{2,1,0:T(8,128)(2,1)S(1)}, bf16[4,64,256]{2,1,0:T(8,128)(2,1)S(1)}, u32[]{:S(2)}, u32[]{:S(2)}) collective-permute-start(bf16[4,64,256]{2,1,0:T(8,128)(2,1)S(1)} %get-tuple-element.263.refs_0_), channel_id=1, source_target_pairs={{0,4},{2,6},{4,0},{6,2},{8,12},{10,14},{12,8},{14,10},{16,20},{18,... | collective-permute-start | bytes 393224 | tf_op jit(solution)/shard_map/ppermute | solution.py:94
  183.7 7.4 %collective-permute-start.44 = (bf16[4,64,256]{2,1,0:T(8,128)(2,1)S(1)}, bf16[4,64,256]{2,1,0:T(8,128)(2,1)S(1)}, u32[]{:S(2)}, u32[]{:S(2)}) collective-permute-start(bf16[4,64,256]{2,1,0:T(8,128)(2,1)S(1)} %get-tuple-element.264.refs_2_), channel_id=1, source_target_pairs={{0,2},{2,0},{4,6},{6,4},{8,10},{10,8},{12,14},{14,12},{16,18},{18,... | collective-permute-start | bytes 393224 | tf_op jit(solution)/shard_map/ppermute | solution.py:94
  191.3 2.7 %collective-permute-start.47 = (bf16[2,2,4,64,512]{4,3,2,1,0:T(8,128)(2,1)S(1)}, bf16[2,2,4,64,512]{4,3,2,1,0:T(8,128)(2,1)S(1)}, u32[]{:S(2)}, u32[]{:S(2)}) collective-permute-start(bf16[2,2,4,64,512]{4,3,2,1,0:T(8,128)(2,1)S(1)} %get-tuple-element.270), channel_id=1, source_target_pairs={{0,1},{1,0},{2,3},{3,2},{4,5},{5,4},{6,7},{7,6},{8,9},{9,8},{10,11... | collective-permute-start | bytes 3145736 | tf_op jit(solution)/shard_map/ppermute | solution.py:94
  191.4 9.1 %collective-permute-start.48 = (bf16[2,4,64,256]{3,2,1,0:T(8,128)(2,1)S(1)}, bf16[2,4,64,256]{3,2,1,0:T(8,128)(2,1)S(1)}, u32[]{:S(2)}, u32[]{:S(2)}) collective-permute-start(bf16[2,4,64,256]{3,2,1,0:T(8,128)(2,1)S(1)} %get-tuple-element.276.refs_0_), channel_id=1, source_target_pairs={{0,2},{2,0},{4,6},{6,4},{8,10},{10,8},{12,14},{14,12},{16,18},{18,... | collective-permute-start | bytes 786440 | tf_op jit(solution)/shard_map/ppermute | solution.py:94
  192.5 8.4 %collective-permute-start.49 = (bf16[2,4,64,256]{3,2,1,0:T(8,128)(2,1)S(1)}, bf16[2,4,64,256]{3,2,1,0:T(8,128)(2,1)S(1)}, u32[]{:S(2)}, u32[]{:S(2)}) collective-permute-start(bf16[2,4,64,256]{3,2,1,0:T(8,128)(2,1)S(1)} %get-tuple-element.277.refs_2_), channel_id=1, source_target_pairs={{0,4},{2,6},{4,0},{6,2},{8,12},{10,14},{12,8},{14,10},{16,20},{18,... | collective-permute-start | bytes 786440 | tf_op jit(solution)/shard_map/ppermute | solution.py:94
  194.0 3.2 %collective-permute-start.46 = (bf16[2,2,4,80,512]{4,3,2,1,0:T(8,128)(2,1)S(1)}, bf16[2,2,4,80,512]{4,3,2,1,0:T(8,128)(2,1)S(1)}, u32[]{:S(2)}, u32[]{:S(2)}) collective-permute-start(bf16[2,2,4,80,512]{4,3,2,1,0:T(8,128)(2,1)S(1)} %get-tuple-element.269), channel_id=1, source_target_pairs={{0,1},{1,0},{2,3},{3,2},{4,5},{5,4},{6,7},{7,6},{8,9},{9,8},{10,11... | collective-permute-start | bytes 3932168 | tf_op jit(solution)/shard_map/ppermute | solution.py:94
  201.0 2.7 %collective-permute-start.50 = (bf16[2,2,4,64,512]{4,3,2,1,0:T(8,128)(2,1)S(1)}, bf16[2,2,4,64,512]{4,3,2,1,0:T(8,128)(2,1)S(1)}, u32[]{:S(2)}, u32[]{:S(2)}) collective-permute-start(bf16[2,2,4,64,512]{4,3,2,1,0:T(8,128)(2,1)S(1)} %get-tuple-element.279), channel_id=1, source_target_pairs={{0,1},{1,0},{2,3},{3,2},{4,5},{5,4},{6,7},{7,6},{8,9},{9,8},{10,11... | collective-permute-start | bytes 3145736 | tf_op jit(solution)/shard_map/ppermute | solution.py:94
  (10 other events, 18.4 us)
where the time goes:
time: 208 us; the launch traced here: 207 us
  Pallas kernels  120 us (58%)
  starting transfers between devices  56.5 us (27%)
  waiting for transfers between devices  20.7 us (10%)
  local copies, waits for them, and re-layouts  8.33 us (4%)
    pallas_call x41, Pallas kernels, run(): pl.pallas_call(wrapped, grid_spec=pltpu.PrefetchScalarGridSpec(num_scalar...  120 us
    ppermute x51, starting transfers between devices, swap(): lax.ppermute(value, name, [(i, i ^ k << shift) for i in range(count)])  56.5 us
    ppermute x51, waiting for transfers between devices, swap(): lax.ppermute(value, name, [(i, i ^ k << shift) for i in range(count)])  20.7 us
    unnamed x46, local copies, waits for them, and re-layouts  7.68 us
  transfers between devices with their start and end apart: 51, of which 16 were waited for; matrix products, arithmetic and copies ran while one was open for 0% of the time, Pallas kernels for 50%

commit v1 on v0

--- a/solution.py
+++ b/solution.py
@@ -1102,7 +1102,7 @@
     )
 
 
-PLAN = ("f t T f", "03 t f", "36 t f", "68 t f t", "w t E F", "Q")
+PLAN = ("f T t f", "04 t f", "46 t f", "68 t f t", "w t E F", "Q")
 
 
 def per_device(

time: 208 us -> 207 us (level)
  transfers between devices with their start and end apart: 51 -> 51, of which waited for: 16 -> 13; matrix products, arithmetic and copies ran while one was open for 0% -> 0% of each run, Pallas kernels for 50% -> 50%
where the time goes in v1:
time: 207 us; the launch traced here: 206 us
  Pallas kernels  119 us (57%)
  starting transfers between devices  57.5 us (28%)
  waiting for transfers between devices  18.9 us (9%)
  local copies, waits for them, and re-layouts  8.04 us (4%)
    pallas_call x41, Pallas kernels, run(): pl.pallas_call(wrapped, grid_spec=pltpu.PrefetchScalarGridSpec(num_scalar...  119 us
    ppermute x51, starting transfers between devices, swap(): lax.ppermute(value, name, [(i, i ^ k << shift) for i in range(count)])  57.5 us
    ppermute x51, waiting for transfers between devices, swap(): lax.ppermute(value, name, [(i, i ^ k << shift) for i in range(count)])  18.9 us
    unnamed x46, local copies, waits for them, and re-layouts  7.4 us
  transfers between devices with their start and end apart: 51, of which 13 were waited for; matrix products, arithmetic and copies ran while one was open for 0% of the time, Pallas kernels for 50%

profile of v1, /device:TPU:0, one launch (start us, length us, event | category | flops | bytes accessed | tf_op | source)
XLA Modules:
  0.0 206.1 jit_solution(4869901690926369171)
XLA Ops:
  0.6 1.0 fusion.2.refs_0_
  1.7 2.2 %copy-done = bf16[256,4,2048]{2,1,0:T(4,128)(2,1)S(1)} copy-done((bf16[256,4,2048]{2,1,0:T(4,128)(2,1)S(1)}, bf16[256,4,2048]{2,1,0:T(4,128)(2,1)}, u32[]{:S(2)}) %copy-start) | copy-done | bytes 4194328
  3.9 0.9 copy-done.9
  4.8 11.5 %scatter_rows.2 = (bf16[2048,256]{1,0:T(8,128)(2,1)}, bf16[2048,512]{1,0:T(8,128)(2,1)}, f32[8,128]{1,0:T(8,128)S(1)}) custom-call(s32[4,2048]{1,0:T(4,128)S(1)} %fusion.2.refs_0_, bf16[256,4,2048]{2,1,0:T(4,128)(2,1)S(1)} %copy-done, bf16[512,256]{1,0:T(8,128)(2,1)S(1)} %copy-done.9), custom_call_target="tpu_custom_call" | custom-call | flops 41999998976 | bytes 126000000 | tf_op jit(solution)/shard_map/scatter_rows/pallas_call | solution.py:66
  17.5 2.2 %copy-done.1 = bf16[256,4,2048]{2,1,0:T(4,128)(2,1)S(1)} copy-done((bf16[256,4,2048]{2,1,0:T(4,128)(2,1)S(1)}, bf16[256,4,2048]{2,1,0:T(4,128)(2,1)}, u32[]{:S(2)}) %copy-start.1) | copy-done | bytes 4194328
  19.7 11.0 %scatter_rows.3 = (bf16[2048,256]{1,0:T(8,128)(2,1)}, f32[2048,512]{1,0:T(8,128)S(1)}, f32[8,128]{1,0:T(8,128)S(1)}) custom-call(s32[4,2048]{1,0:T(4,128)S(1)} %fusion.2.refs_0_, bf16[256,4,2048]{2,1,0:T(4,128)(2,1)S(1)} %copy-done.1, bf16[512,256]{1,0:T(8,128)(2,1)S(1)} %copy-done.10, f32[8,128]{1,0:T(8,128)S(1)} %get-tuple-element.148.refs_3_), custom_call_target="tpu_custom_call" | custom-call | flops 41999998976 | bytes 126000000 | tf_op jit(solution)/shard_map/scatter_rows/pallas_call | solution.py:66
  31.2 2.6 %collective-permute-start.1 = (bf16[2,4,128,256]{3,2,1,0:T(8,128)(2,1)S(1)}, bf16[2,4,128,256]{3,2,1,0:T(8,128)(2,1)S(1)}, u32[]{:S(2)}, u32[]{:S(2)}) collective-permute-start(bf16[2,4,128,256]{3,2,1,0:T(8,128)(2,1)S(1)} %get-tuple-element.156), channel_id=1, source_target_pairs={{0,2},{2,0},{4,6},{6,4},{8,10},{10,8},{12,14},{14,12},{16,18},{18,... | collective-permute-start | bytes 1572872 | tf_op jit(solution)/shard_map/ppermute | solution.py:94
  33.8 1.5 collective-permute-start.2
  35.3 11.2 %attn_forward.1 = (bf16[1024,512]{1,0:T(8,128)(2,1)S(1)}, bf16[1024,1536]{1,0:T(8,128)(2,1)}, bf16[1024,512]{1,0:T(8,128)(2,1)S(1)}, f32[1024,512]{1,0:T(8,128)S...) custom-call(bf16[128,8,512]{2,1,0:T(8,128)(2,1)S(1)} %copy-done.6, ...), custom_call_target="tpu_custom_call" | custom-call | flops 35999997952 | bytes 108000000 | tf_op jit(solution)/shard_map/attn_forward/pallas_call | solution.py:66
  46.6 1.2 collective-permute-done.2.refs_3_
  48.0 1.6 collective-permute-start.3
  50.2 8.0 %ffn_forward.2 = (f32[1024,1024]{1,0:T(8,128)}, bf16[128,1024]{1,0:T(8,128)(2,1)S(1)}, f32[128,512]{1,0:T(8,128)S(1)}, f32[8,128]{1,0:T(8,128)S(1)}) custom-call(s32[1024,1]{1,0:T(8,128)S(1)} %broadcast_in_dim_reshape.8.refs_2_.refs_0_.refs_1_, s32[128,1]{1,0:T(8,128)S(1)} %copy.32.refs_1_, f32[1024,512]{1,0:T(8,128)S(1)} %get-tuple-element.153.refs_2_.refs_4_, ...), custom_call_target="tpu_custom_call" | custom-call | flops 20999999488 | bytes 63000000 | tf_op jit(solution)/shard_map/ffn_forward/pallas_call | solution.py:66
  58.3 1.7 collective-permute-start.5
  59.9 2.6 %collective-permute-start.6 = (bf16[128,512]{1,0:T(8,128)(2,1)S(1)}, bf16[128,512]{1,0:T(8,128)(2,1)S(1)}, u32[]{:S(2)}, u32[]{:S(2)}) collective-permute-start(bf16[128,512]{1,0:T(8,128)(2,1)S(1)} %get-tuple-element.171), channel_id=1, source_target_pairs={{0,16},{2,18},{4,20},{6,22},{8,24},{10,26},{12,28},{14,30},{16,0},... | collective-permute-start | bytes 393224 | tf_op jit(solution)/shard_map/ppermute | solution.py:94
  62.7 8.0 %ffn_forward.3 = (f32[1024,1024]{1,0:T(8,128)}, bf16[128,1024]{1,0:T(8,128)(2,1)S(1)}, bf16[128,512]{1,0:T(8,128)(2,1)S(1)}, f32[8,128]{1,0:T(8,128)S(1)}) custom-call(s32[1024,1]{1,0:T(8,128)S(1)} %broadcast_in_dim_reshape.8.refs_2_.refs_0_.refs_1_, s32[128,1]{1,0:T(8,128)S(1)} %copy.32.refs_1_, f32[128,512]{1,0:T(8,128)S(1)} %get-tuple-element.161.refs_2_, ...), custom_call_target="tpu_custom_call" | custom-call | flops 20999999488 | bytes 63000000 | tf_op jit(solution)/shard_map/ffn_forward/pallas_call | solution.py:66
  70.7 1.6 collective-permute-done.6.refs_2_
  72.4 2.5 %collective-permute-start.10 = (bf16[128,512]{1,0:T(8,128)(2,1)S(1)}, bf16[128,512]{1,0:T(8,128)(2,1)S(1)}, u32[]{:S(2)}, u32[]{:S(2)}) collective-permute-start(bf16[128,512]{1,0:T(8,128)(2,1)S(1)} %get-tuple-element.175.refs_0_), channel_id=1, source_target_pairs={{0,24},{2,26},{4,28},{6,30},{8,16},{10,18},{12,20},{14,22},{16,8},... | collective-permute-start | bytes 393224 | tf_op jit(solution)/shard_map/ppermute | solution.py:94
  74.9 1.1 collective-permute-start.8
  76.0 0.8 collective-permute-start.9
  76.9 2.5 %tall_weight.1 = (f32[16,64,512]{2,1,0:T(8,128)S(1)}, bf16[16,64,512]{2,1,0:T(8,128)(2,1)S(1)}, f32[8,128]{1,0:T(8,128)S(1)}) custom-call(s32[32]{0:T(128)S(1)} %iota_xor_fusion.refs_0_, bf16[128,1024]{1,0:T(8,128)(2,1)S(1)} %get-tuple-element.179.refs_1_, bf16[128,1024]{1,0:T(8,128)(2,1)S(1)} %get-tuple-element.180.refs_2_, ...), custom_call_target="tpu_custom_call" | custom-call | flops 8999999488 | bytes 27000000 | tf_op jit(solution)/shard_map/tall_weight/pallas_call | solution.py:66
  79.5 0.8 copy-done.17
  80.3 6.8 %ffn_back.1 = (bf16[1024,2048]{1,0:T(8,128)(2,1)S(1)}, f32[1024,512]{1,0:T(8,128)S(1)}, bf16[1024,512]{1,0:T(8,128)(2,1)S(1)}, f32[1,512]{1,0:T(1,128)S(1)}, f32[8,128]{1,0:T(8,128)S(1)}) custom-call(f32[128,512]{1,0:T(8,128)S(1)} %get-tuple-element.176.refs_0_, s32[1024,1]{1,0:T(8,128)S(1)} %broadcast_in_dim_reshape.8.refs_2_.refs_0_.refs_1_, ...), custom_call_target="tpu_custom_call" | custom-call | flops 44999999488 | bytes 135000000 | tf_op jit(solution)/shard_map/ffn_back/pallas_call | solution.py:66
  87.2 1.6 collective-permute-start.11
  89.4 4.4 %wide_weight.1 = (f32[16,64,512]{2,1,0:T(8,128)S(1)}, bf16[16,64,512]{2,1,0:T(8,128)(2,1)S(1)}, f32[8,128]{1,0:T(8,128)S(1)}) custom-call(s32[32]{0:T(128)S(1)} %iota_xor_fusion.refs_0_, bf16[1024,512]{1,0:T(8,128)(2,1)S(1)} %get-tuple-element.154.refs_3_.refs_1_, bf16[1024,2048]{1,0:T(8,128)(2,1)S(1)} %get-tuple-element.186.refs_2_, ...), custom_call_target="tpu_custom_call" | custom-call | flops 24000000000 | bytes 72000000 | tf_op jit(solution)/shard_map/wide_weight/pallas_call | solution.py:66
  93.9 1.2 collective-permute-done.11.refs_1_
  95.1 1.3 collective-permute-done.12.refs_3_
  97.1 1.0 collective-permute-start.14
  98.3 6.3 %heads_back.1 = (bf16[1024,1536]{1,0:T(8,128)(2,1)S(1)}, f32[8,128]{1,0:T(8,128)S(1)}) custom-call(s32[1024,1]{1,0:T(8,128)S(1)} %broadcast_in_dim_reshape.8.refs_2_.refs_0_.refs_1_, bf16[512,512]{1,0:T(8,128)(2,1)S(1)} %copy-done.8, bf16[1024,1536]{1,0:T(8,128)(2,1)S(1)} %copy-done.20, bf16[1024,512]{1,0:T(8,128)(2,1)S(1)} %get-tuple-element.193.refs_3_.refs_4_, ...), custom_call_target="tpu_custom_call" | custom-call | flops 38999998464 | bytes 117000000 | tf_op jit(solution)/shard_map/heads_back/pallas_call | solution.py:66
  104.9 0.8 collective-permute-start.18
  105.8 1.5 collective-permute-start.19
  107.3 4.3 %two_weights.1 = (f32[16,64,512]{2,1,0:T(8,128)S(1)}, bf16[16,64,512]{2,1,0:T(8,128)(2,1)S(1)}, f32[8,128]{1,0:T(8,128)S(1)}) custom-call(s32[32]{0:T(128)S(1)} %iota_xor_fusion.refs_0_, bf16[1024,512]{1,0:T(8,128)(2,1)S(1)} %get-tuple-element.191.refs_1_, bf16[1024,1536]{1,0:T(8,128)(2,1)S(1)} %get-tuple-element.195.refs_2_.refs_5_, ...), custom_call_target="tpu_custom_call" | custom-call | flops 15000000512 | bytes 45000000 | tf_op jit(solution)/shard_map/two_weights/pallas_call | solution.py:66
  113.7 6.8 %attn_back.1 = (f32[128,8,512]{2,1,0:T(8,128)}, f32[32,512]{1,0:T(8,128)S(1)}, f32[8,128]{1,0:T(8,128)S(1)}) custom-call(bf16[128,8,512]{2,1,0:T(8,128)(2,1)S(1)} %copy-done.7, s32[1024,1]{1,0:T(8,128)S(1)} %broadcast_in_dim_reshape.9.refs_1_, f32[16,512]{1,0:T(8,128)S(1)} %copy-done.12, f32[1,512]{1,0:T(1,128)S(1)} %bitcast.38, ...), custom_call_target="tpu_custom_call" | custom-call | flops 27000000512 | bytes 81000000 | tf_op jit(solution)/shard_map/attn_back/pallas_call | solution.py:66
  121.6 1.1 collective-permute-start.21
  122.7 3.3 %table_and_grad.1 = (bf16[256,4096]{1,0:T(8,128)(2,1)S(1)}, f32[512,256]{1,0:T(8,128)S(1)}, f32[8,128]{1,0:T(8,128)S(1)}) custom-call(bf16[2048,512]{1,0:T(8,128)(2,1)S(1)} %bitcast.24, bf16[2048,512]{1,0:T(8,128)(2,1)S(1)} %bitcast.25, bf16[512,256]{1,0:T(8,128)(2,1)S(1)} %copy-done.10, bf16[2048,256]{1,0:T(8,128)(2,1)S(1)} %copy-done.19, ...), custom_call_target="tpu_custom_call" | custom-call | flops 15000000512 | bytes 45000000 | tf_op jit(solution)/shard_map/table_and_grad/pallas_call | solution.py:66
  126.2 1.0 collective-permute-start.26
  127.2 1.5 collective-permute-start.27
  128.7 0.9 collective-permute-done.21.refs_3_
  129.7 1.1 collective-permute-start.23
  130.9 2.0 collective-permute-start.24
  132.8 1.4 collective-permute-start.25
  134.2 10.6 %lookup.3 = (bf16[256,4,2048]{2,1,0:T(4,128)(2,1)}, f32[8,128]{1,0:T(8,128)S(1)}) custom-call(s32[4,2048]{1,0:T(4,128)S(1)} %fusion.2.refs_0_, bf16[256,4096]{1,0:T(8,128)(2,1)S(1)} %get-tuple-element.216.refs_1_, f32[8,128]{1,0:T(8,128)S(1)} %get-tuple-element.234.refs_2_), custom_call_target="tpu_custom_call" | custom-call | flops 35999997952 | bytes 108000000 | tf_op jit(solution)/shard_map/lookup/pallas_call | solution.py:66
  145.7 2.4 %collective-permute-start.29 = (bf16[128,512]{1,0:T(8,128)(2,1)S(1)}, bf16[128,512]{1,0:T(8,128)(2,1)S(1)}, u32[]{:S(2)}, u32[]{:S(2)}) collective-permute-start(bf16[128,512]{1,0:T(8,128)(2,1)S(1)} %get-tuple-element.237.refs_0_), channel_id=1, source_target_pairs={{0,16},{2,18},{4,20},{6,22},{8,24},{10,26},{12,28},{14,30},{16,0},... | collective-permute-start | bytes 393224 | tf_op jit(solution)/shard_map/ppermute | solution.py:94
  148.1 1.4 collective-permute-start.30
  149.5 1.3 collective-permute-start.31
  150.8 1.8 collective-permute-start.32
  152.5 5.7 %lookup.4 = (bf16[256,4,2048]{2,1,0:T(4,128)(2,1)}, f32[8,128]{1,0:T(8,128)S(1)}) custom-call(s32[4,2048]{1,0:T(4,128)S(1)} %fusion.2.refs_0_, bf16[256,4096]{1,0:T(8,128)(2,1)S(1)} %get-tuple-element.216.refs_1_, f32[8,128]{1,0:T(8,128)S(1)} %get-tuple-element.243.refs_2_, ...), custom_call_target="tpu_custom_call", output_to_operand_aliasing={{0}: (3, {})} | custom-call | flops 17999998976 | bytes 54000000 | tf_op jit(solution)/shard_map/lookup/pallas_call | solution.py:66
  158.4 3.0 %collective-permute-start.36 = (bf16[64,512]{1,0:T(8,128)(2,1)S(1)}, bf16[64,512]{1,0:T(8,128)(2,1)S(1)}, u32[]{:S(2)}, u32[]{:S(2)}) collective-permute-start(bf16[64,512]{1,0:T(8,128)(2,1)S(1)} %get-tuple-element.255), channel_id=1, source_target_pairs={{0,16},{2,18},{4,20},{6,22},{8,24},{10,26},{12,28},{14,30},{16,0},... | collective-permute-start | bytes 196616 | tf_op jit(solution)/shard_map/ppermute | solution.py:94
  161.4 1.4 collective-permute-start.37
  163.8 5.7 %lookup.5 = (bf16[256,4,2048]{2,1,0:T(4,128)(2,1)}, f32[8,128]{1,0:T(8,128)S(1)}) custom-call(s32[4,2048]{1,0:T(4,128)S(1)} %fusion.2.refs_0_, bf16[256,4096]{1,0:T(8,128)(2,1)S(1)} %get-tuple-element.216.refs_1_, f32[8,128]{1,0:T(8,128)S(1)} %get-tuple-element.247.refs_2_, ...), custom_call_target="tpu_custom_call", output_to_operand_aliasing={{0}: (3, {})} | custom-call | flops 17999998976 | bytes 54000000 | tf_op jit(solution)/shard_map/lookup/pallas_call | solution.py:66
  170.0 1.1 collective-permute-start.39
  171.5 1.4 collective-permute-start.38
  172.9 3.0 %collective-permute-start.41 = (bf16[64,512]{1,0:T(8,128)(2,1)S(1)}, bf16[64,512]{1,0:T(8,128)(2,1)S(1)}, u32[]{:S(2)}, u32[]{:S(2)}) collective-permute-start(bf16[64,512]{1,0:T(8,128)(2,1)S(1)} %get-tuple-element.261.refs_0_), channel_id=1, source_target_pairs={{0,16},{2,18},{4,20},{6,22},{8,24},{10,26},{12,28},{14,30},{16,0},... | collective-permute-start | bytes 196616 | tf_op jit(solution)/shard_map/ppermute | solution.py:94
  175.9 1.9 collective-permute-start.42
  177.8 3.0 %collective-permute-done.41.refs_2_ = bf16[64,512]{1,0:T(8,128)(2,1)S(1)} collective-permute-done((bf16[64,512]{1,0:T(8,128)(2,1)S(1)}, bf16[64,512]{1,0:T(8,128)(2,1)S(1)}, u32[]{:S(2)}, u32[]{:S(2)}) %collective-permute-start.41) | collective-permute-done | bytes 65568 | tf_op jit(solution)/shard_map/ppermute | solution.py:94
  180.8 1.3 collective-permute-done.42.refs_3_
  182.7 1.3 collective-permute-start.44
  184.1 0.8 exchange.42
  184.9 4.8 %collective-permute-done.43.refs_1_ = bf16[4,64,256]{2,1,0:T(8,128)(2,1)S(1)} collective-permute-done((bf16[4,64,256]{2,1,0:T(8,128)(2,1)S(1)}, bf16[4,64,256]{2,1,0:T(8,128)(2,1)S(1)}, u32[]{:S(2)}, u32[]{:S(2)}) %collective-permute-start.43) | collective-permute-done | bytes 131104 | tf_op jit(solution)/shard_map/ppermute | solution.py:94
  190.0 1.4 collective-permute-start.48
  191.4 1.7 collective-permute-start.49
  193.2 3.2 %unpack.2 = (f32[2048,512]{1,0:T(8,128)}, f32[8,128]{1,0:T(8,128)S(1)}) custom-call(s32[32]{0:T(128)S(1)} %iota_xor_fusion.refs_0_, bf16[16,64,512]{2,1,0:T(8,128)(2,1)S(1)} %bitcast.31, bf16[16,64,512]{2,1,0:T(8,128)(2,1)S(1)} %bitcast.32, f32[8,128]{1,0:T(8,128)S(1)} %get-tuple-element.271.refs_3_), custom_call_target="tpu_custom_call" | custom-call | flops 15000000512 | bytes 45000000 | tf_op jit(solution)/shard_map/unpack/pallas_call | solution.py:66
  196.4 3.2 %unpack.3 = (f32[512,2048]{1,0:T(8,128)}, f32[16,512]{1,0:T(8,128)}, f32[1,512]{1,0:T(1,128)}, f32[1,512]{1,0:T(1,128)}, f32[8,128]{1,0:T(8,128)S(1)}) custom-call(s32[32]{0:T(128)S(1)} %iota_xor_fusion.refs_0_, bf16[16,80,512]{2,1,0:T(8,128)(2,1)S(1)} %bitcast.26, bf16[16,80,512]{2,1,0:T(8,128)(2,1)S(1)} %bitcast.27, f32[8,128]{1,0:T(8,128)S(1)} %get-tuple-element.272.refs_3_), custom_call_target="tpu_custom_call" | custom-call | flops 15000000512 | bytes 45000000 | tf_op jit(solution)/shard_map/unpack/pallas_call | solution.py:66
  200.3 2.3 %collective-permute-done.50 = bf16[2,2,4,64,512]{4,3,2,1,0:T(8,128)(2,1)S(1)} collective-permute-done((bf16[2,2,4,64,512]{4,3,2,1,0:T(8,128)(2,1)S(1)}, bf16[2,2,4,64,512]{4,3,2,1,0:T(8,128)(2,1)S(1)}, u32[]{:S(2)}, u32[]{:S(2)}) %collective-permute-start.50) | collective-permute-done | bytes 1048608 | tf_op jit(solution)/shard_map/ppermute | solution.py:94
  202.6 3.5 %unpack_two.1 = (f32[512,1536]{1,0:T(8,128)}, f32[512,512]{1,0:T(8,128)}, f32[8,128]{1,0:T(8,128)}) custom-call(s32[32]{0:T(128)S(1)} %iota_xor_fusion.refs_0_, bf16[16,64,512]{2,1,0:T(8,128)(2,1)S(1)} %bitcast.33, bf16[16,64,512]{2,1,0:T(8,128)(2,1)S(1)} %bitcast.34, f32[8,128]{1,0:T(8,128)S(1)} %get-tuple-element.280.refs_3_), custom_call_target="tpu_custom_call" | custom-call | flops 15000000512 | bytes 45000000 | tf_op jit(solution)/shard_map/unpack_two/pallas_call | solution.py:66
  (133 shorter events, 13.0 us)
Async XLA Ops:
  4.8 11.9 %copy-start.21 = (s32[128]{0:T(128)S(1)}, s32[128]{0:T(128)}, u32[]{:S(2)}) copy-start(s32[128]{0:T(128)} %param.14) | copy-start | bytes 1540
  4.8 12.2 %copy-start.22 = (s32[128]{0:T(128)S(1)}, s32[128]{0:T(128)}, u32[]{:S(2)}) copy-start(s32[128]{0:T(128)} %param.15) | copy-start | bytes 1540
  4.8 12.6 %copy-start.10 = (bf16[512,256]{1,0:T(8,128)(2,1)S(1)}, bf16[512,256]{1,0:T(8,128)(2,1)}, u32[]{:S(2)}) copy-start(bf16[512,256]{1,0:T(8,128)(2,1)} %refs_2_.7) | copy-start | bytes 786436
  16.3 14.4 %collective-permute-start = (bf16[2,2,4,128,512]{4,3,2,1,0:T(8,128)(2,1)}, bf16[2,2,4,128,512]{4,3,2,1,0:T(8,128)(2,1)S(1)}, u32[]{:S(2)}, u32[]{:S(2)}) collective-permute-start(bf16[2,2,4,128,512]{4,3,2,1,0:T(8,128)(2,1)} %bitcast.4), channel_id=1, source_target_pairs={{0,1},{1,0},{2,3},{3,2},{4,5},{5,4},{6,7},{7,6},{8,9},{9,8},{10,11... | collective-permute-start | bytes 6291464 | tf_op jit(solution)/shard_map/ppermute | solution.py:94
  30.7 4.6 %copy-start.4 = (bf16[512,1536]{1,0:T(8,128)(2,1)S(1)}, bf16[512,1536]{1,0:T(8,128)(2,1)}, u32[]{:S(2)}) copy-start(bf16[512,1536]{1,0:T(8,128)(2,1)} %refs_4_.5) | copy-start | bytes 4718596
  30.7 4.6 %copy-start.6 = (bf16[128,8,512]{2,1,0:T(8,128)(2,1)S(1)}, bf16[128,8,512]{2,1,0:T(8,128)(2,1)}, u32[]{:S(2)}) copy-start(bf16[128,8,512]{2,1,0:T(8,128)(2,1)} %refs_0_.3) | copy-start | bytes 3145732
  30.7 4.6 %copy-start.8 = (bf16[512,512]{1,0:T(8,128)(2,1)S(1)}, bf16[512,512]{1,0:T(8,128)(2,1)}, u32[]{:S(2)}) copy-start(bf16[512,512]{1,0:T(8,128)(2,1)} %refs_1_.5) | copy-start | bytes 1572868
  30.7 4.6 %copy-start.11 = (f32[16,512]{1,0:T(8,128)S(1)}, f32[16,512]{1,0:T(8,128)}, u32[]{:S(2)}) copy-start(f32[16,512]{1,0:T(8,128)} %refs_2_.6) | copy-start | bytes 98308
  30.7 4.6 %copy-start.13 = (f32[512]{0:T(512)S(1)}, f32[512]{0:T(512)}, u32[]{:S(2)}) copy-start(f32[512]{0:T(512)} %param.18) | copy-start | bytes 6148
  30.7 4.6 %copy-start.14 = (f32[512]{0:T(512)S(1)}, f32[512]{0:T(512)}, u32[]{:S(2)}) copy-start(f32[512]{0:T(512)} %param.17) | copy-start | bytes 6148
  31.2 15.4 %collective-permute-start.1 = (bf16[2,4,128,256]{3,2,1,0:T(8,128)(2,1)S(1)}, bf16[2,4,128,256]{3,2,1,0:T(8,128)(2,1)S(1)}, u32[]{:S(2)}, u32[]{:S(2)}) collective-permute-start(bf16[2,4,128,256]{3,2,1,0:T(8,128)(2,1)S(1)} %get-tuple-element.156), channel_id=1, source_target_pairs={{0,2},{2,0},{4,6},{6,4},{8,10},{10,8},{12,14},{14,12},{16,18},{18,... | collective-permute-start | bytes 1572872 | tf_op jit(solution)/shard_map/ppermute | solution.py:94
  33.8 14.1 %collective-permute-start.2 = (bf16[2,4,128,256]{3,2,1,0:T(8,128)(2,1)S(1)}, bf16[2,4,128,256]{3,2,1,0:T(8,128)(2,1)S(1)}, u32[]{:S(2)}, u32[]{:S(2)}) collective-permute-start(bf16[2,4,128,256]{3,2,1,0:T(8,128)(2,1)S(1)} %get-tuple-element.158), channel_id=1, source_target_pairs={{0,4},{2,6},{4,0},{6,2},{8,12},{10,14},{12,8},{14,10},{16,20},{18,... | collective-permute-start | bytes 1572872 | tf_op jit(solution)/shard_map/ppermute | solution.py:94
  47.8 2.3 %copy-start.2 = (bf16[512,2048]{1,0:T(8,128)(2,1)S(1)}, bf16[512,2048]{1,0:T(8,128)(2,1)}, u32[]{:S(2)}) copy-start(bf16[512,2048]{1,0:T(8,128)(2,1)} %refs_6_.3) | copy-start | bytes 6291460
  47.8 2.3 %copy-start.3 = (bf16[2048,512]{1,0:T(8,128)(2,1)S(1)}, bf16[2048,512]{1,0:T(8,128)(2,1)}, u32[]{:S(2)}) copy-start(bf16[2048,512]{1,0:T(8,128)(2,1)} %refs_7_.3) | copy-start | bytes 6291460
  48.0 10.1 %collective-permute-start.3 = (bf16[4,128,256]{2,1,0:T(8,128)(2,1)S(1)}, bf16[4,128,256]{2,1,0:T(8,128)(2,1)S(1)}, u32[]{:S(2)}, u32[]{:S(2)}) collective-permute-start(bf16[4,128,256]{2,1,0:T(8,128)(2,1)S(1)} %get-tuple-element.163), channel_id=1, source_target_pairs={{0,4},{2,6},{4,0},{6,2},{8,12},{10,14},{12,8},{14,10},{16,20},{18,... | collective-permute-start | bytes 786440 | tf_op jit(solution)/shard_map/ppermute | solution.py:94
  49.6 8.5 %collective-permute-start.4 = (bf16[4,128,256]{2,1,0:T(8,128)(2,1)S(1)}, bf16[4,128,256]{2,1,0:T(8,128)(2,1)S(1)}, u32[]{:S(2)}, u32[]{:S(2)}) collective-permute-start(bf16[4,128,256]{2,1,0:T(8,128)(2,1)S(1)} %get-tuple-element.165), channel_id=1, source_target_pairs={{0,2},{2,0},{4,6},{6,4},{8,10},{10,8},{12,14},{14,12},{16,18},{18,... | collective-permute-start | bytes 786440 | tf_op jit(solution)/shard_map/ppermute | solution.py:94
  58.3 12.4 %collective-permute-start.5 = (bf16[128,512]{1,0:T(8,128)(2,1)S(1)}, bf16[128,512]{1,0:T(8,128)(2,1)S(1)}, u32[]{:S(2)}, u32[]{:S(2)}) collective-permute-start(bf16[128,512]{1,0:T(8,128)(2,1)S(1)} %get-tuple-element.170), channel_id=1, source_target_pairs={{0,8},{2,10},{4,12},{6,14},{8,0},{10,2},{12,4},{14,6},{16,24},{18,... | collective-permute-start | bytes 393224 | tf_op jit(solution)/shard_map/ppermute | solution.py:94
  59.9 12.4 %collective-permute-start.6 = (bf16[128,512]{1,0:T(8,128)(2,1)S(1)}, bf16[128,512]{1,0:T(8,128)(2,1)S(1)}, u32[]{:S(2)}, u32[]{:S(2)}) collective-permute-start(bf16[128,512]{1,0:T(8,128)(2,1)S(1)} %get-tuple-element.171), channel_id=1, source_target_pairs={{0,16},{2,18},{4,20},{6,22},{8,24},{10,26},{12,28},{14,30},{16,0},... | collective-permute-start | bytes 393224 | tf_op jit(solution)/shard_map/ppermute | solution.py:94
  62.5 9.8 %collective-permute-start.7 = (bf16[128,512]{1,0:T(8,128)(2,1)S(1)}, bf16[128,512]{1,0:T(8,128)(2,1)S(1)}, u32[]{:S(2)}, u32[]{:S(2)}) collective-permute-start(bf16[128,512]{1,0:T(8,128)(2,1)S(1)} %get-tuple-element.172), channel_id=1, source_target_pairs={{0,24},{2,26},{4,28},{6,30},{8,16},{10,18},{12,20},{14,22},{16,8},... | collective-permute-start | bytes 393224 | tf_op jit(solution)/shard_map/ppermute | solution.py:94
  72.4 14.8 %collective-permute-start.10 = (bf16[128,512]{1,0:T(8,128)(2,1)S(1)}, bf16[128,512]{1,0:T(8,128)(2,1)S(1)}, u32[]{:S(2)}, u32[]{:S(2)}) collective-permute-start(bf16[128,512]{1,0:T(8,128)(2,1)S(1)} %get-tuple-element.175.refs_0_), channel_id=1, source_target_pairs={{0,24},{2,26},{4,28},{6,30},{8,16},{10,18},{12,20},{14,22},{16,8},... | collective-permute-start | bytes 393224 | tf_op jit(solution)/shard_map/ppermute | solution.py:94
  74.9 12.2 %collective-permute-start.8 = (bf16[128,512]{1,0:T(8,128)(2,1)S(1)}, bf16[128,512]{1,0:T(8,128)(2,1)S(1)}, u32[]{:S(2)}, u32[]{:S(2)}) collective-permute-start(bf16[128,512]{1,0:T(8,128)(2,1)S(1)} %get-tuple-element.175.refs_0_), channel_id=1, source_target_pairs={{0,8},{2,10},{4,12},{6,14},{8,0},{10,2},{12,4},{14,6},{16,24},{18,... | collective-permute-start | bytes 393224 | tf_op jit(solution)/shard_map/ppermute | solution.py:94
  76.0 11.2 %collective-permute-start.9 = (bf16[128,512]{1,0:T(8,128)(2,1)S(1)}, bf16[128,512]{1,0:T(8,128)(2,1)S(1)}, u32[]{:S(2)}, u32[]{:S(2)}) collective-permute-start(bf16[128,512]{1,0:T(8,128)(2,1)S(1)} %get-tuple-element.175.refs_0_), channel_id=1, source_target_pairs={{0,16},{2,18},{4,20},{6,22},{8,24},{10,26},{12,28},{14,30},{16,0},... | collective-permute-start | bytes 393224 | tf_op jit(solution)/shard_map/ppermute | solution.py:94
  76.8 2.6 %copy-start.16 = (f32[1024,1024]{1,0:T(8,128)S(1)}, f32[1024,1024]{1,0:T(8,128)}, u32[]{:S(2)}) copy-start(f32[1024,1024]{1,0:T(8,128)} %get-tuple-element.177.refs_2_) | copy-start | bytes 12582916
  76.9 3.5 %copy-start.17 = (f32[1024,1024]{1,0:T(8,128)S(1)}, f32[1024,1024]{1,0:T(8,128)}, u32[]{:S(2)}) copy-start(f32[1024,1024]{1,0:T(8,128)} %get-tuple-element.178.refs_3_) | copy-start | bytes 12582916
  79.4 25.2 %collective-permute-start.15 = (bf16[2,2,4,64,512]{4,3,2,1,0:T(8,128)(2,1)S(1)}, bf16[2,2,4,64,512]{4,3,2,1,0:T(8,128)(2,1)S(1)}, u32[]{:S(2)}, u32[]{:S(2)}) collective-permute-start(bf16[2,2,4,64,512]{4,3,2,1,0:T(8,128)(2,1)S(1)} %bitcast.28), channel_id=1, source_target_pairs={{0,1},{1,0},{2,3},{3,2},{4,5},{5,4},{6,7},{7,6},{8,9},{9,8},{10,11... | collective-permute-start | bytes 3145736 | tf_op jit(solution)/shard_map/ppermute | solution.py:94
  87.2 7.9 %collective-permute-start.11 = (bf16[4,128,256]{2,1,0:T(8,128)(2,1)S(1)}, bf16[4,128,256]{2,1,0:T(8,128)(2,1)S(1)}, u32[]{:S(2)}, u32[]{:S(2)}) collective-permute-start(bf16[4,128,256]{2,1,0:T(8,128)(2,1)S(1)} %get-tuple-element.184.refs_0_), channel_id=1, source_target_pairs={{0,4},{2,6},{4,0},{6,2},{8,12},{10,14},{12,8},{14,10},{16,20},{18,... | collective-permute-start | bytes 786440 | tf_op jit(solution)/shard_map/ppermute | solution.py:94
  88.8 7.6 %collective-permute-start.12 = (bf16[4,128,256]{2,1,0:T(8,128)(2,1)S(1)}, bf16[4,128,256]{2,1,0:T(8,128)(2,1)S(1)}, u32[]{:S(2)}, u32[]{:S(2)}) collective-permute-start(bf16[4,128,256]{2,1,0:T(8,128)(2,1)S(1)} %get-tuple-element.185.refs_2_), channel_id=1, source_target_pairs={{0,2},{2,0},{4,6},{6,4},{8,10},{10,8},{12,14},{14,12},{16,18},{18,... | collective-permute-start | bytes 786440 | tf_op jit(solution)/shard_map/ppermute | solution.py:94
  93.8 10.8 %collective-permute-start.16 = (bf16[2,2,4,64,512]{4,3,2,1,0:T(8,128)(2,1)S(1)}, bf16[2,2,4,64,512]{4,3,2,1,0:T(8,128)(2,1)S(1)}, u32[]{:S(2)}, u32[]{:S(2)}) collective-permute-start(bf16[2,2,4,64,512]{4,3,2,1,0:T(8,128)(2,1)S(1)} %bitcast.30), channel_id=1, source_target_pairs={{0,1},{1,0},{2,3},{3,2},{4,5},{5,4},{6,7},{7,6},{8,9},{9,8},{10,11... | collective-permute-start | bytes 3145736 | tf_op jit(solution)/shard_map/ppermute | solution.py:94
  96.5 15.2 %collective-permute-start.13 = (bf16[2,4,128,256]{3,2,1,0:T(8,128)(2,1)S(1)}, bf16[2,4,128,256]{3,2,1,0:T(8,128)(2,1)S(1)}, u32[]{:S(2)}, u32[]{:S(2)}) collective-permute-start(bf16[2,4,128,256]{3,2,1,0:T(8,128)(2,1)S(1)} %get-tuple-element.189.refs_0_), channel_id=1, source_target_pairs={{0,2},{2,0},{4,6},{6,4},{8,10},{10,8},{12,14},{14,12},{16,18},{18,... | collective-permute-start | bytes 1572872 | tf_op jit(solution)/shard_map/ppermute | solution.py:94
  97.1 14.9 %collective-permute-start.14 = (bf16[2,4,128,256]{3,2,1,0:T(8,128)(2,1)S(1)}, bf16[2,4,128,256]{3,2,1,0:T(8,128)(2,1)S(1)}, u32[]{:S(2)}, u32[]{:S(2)}) collective-permute-start(bf16[2,4,128,256]{3,2,1,0:T(8,128)(2,1)S(1)} %get-tuple-element.190.refs_2_), channel_id=1, source_target_pairs={{0,4},{2,6},{4,0},{6,2},{8,12},{10,14},{12,8},{14,10},{16,20},{18,... | collective-permute-start | bytes 1572872 | tf_op jit(solution)/shard_map/ppermute | solution.py:94
  104.9 15.5 %collective-permute-start.18 = (bf16[2,4,64,512]{3,2,1,0:T(8,128)(2,1)S(1)}, bf16[2,4,64,512]{3,2,1,0:T(8,128)(2,1)S(1)}, u32[]{:S(2)}, u32[]{:S(2)}) collective-permute-start(bf16[2,4,64,512]{3,2,1,0:T(8,128)(2,1)S(1)} %get-tuple-element.208), channel_id=1, source_target_pairs={{0,2},{2,0},{4,6},{6,4},{8,10},{10,8},{12,14},{14,12},{16,18},{18,... | collective-permute-start | bytes 1572872 | tf_op jit(solution)/shard_map/ppermute | solution.py:94
  105.8 15.0 %collective-permute-start.19 = (bf16[2,4,64,512]{3,2,1,0:T(8,128)(2,1)S(1)}, bf16[2,4,64,512]{3,2,1,0:T(8,128)(2,1)S(1)}, u32[]{:S(2)}, u32[]{:S(2)}) collective-permute-start(bf16[2,4,64,512]{3,2,1,0:T(8,128)(2,1)S(1)} %get-tuple-element.210), channel_id=1, source_target_pairs={{0,4},{2,6},{4,0},{6,2},{8,12},{10,14},{12,8},{14,10},{16,20},{18,... | collective-permute-start | bytes 1572872 | tf_op jit(solution)/shard_map/ppermute | solution.py:94
  112.2 10.6 %collective-permute-start.17 = (bf16[2,2,4,128,512]{4,3,2,1,0:T(8,128)(2,1)S(1)}, bf16[2,2,4,128,512]{4,3,2,1,0:T(8,128)(2,1)S(1)}, u32[]{:S(2)}, u32[]{:S(2)}) collective-permute-start(bf16[2,2,4,128,512]{4,3,2,1,0:T(8,128)(2,1)S(1)} %get-tuple-element.204), channel_id=1, source_target_pairs={{0,1},{1,0},{2,3},{3,2},{4,5},{5,4},{6,7},{7,6},{8,9},{9,8},{10,11... | collective-permute-start | bytes 6291464 | tf_op jit(solution)/shard_map/ppermute | solution.py:94
  112.2 13.8 %collective-permute-start.22 = (bf16[2,2,4,64,512]{4,3,2,1,0:T(8,128)(2,1)S(1)}, bf16[2,2,4,64,512]{4,3,2,1,0:T(8,128)(2,1)S(1)}, u32[]{:S(2)}, u32[]{:S(2)}) collective-permute-start(bf16[2,2,4,64,512]{4,3,2,1,0:T(8,128)(2,1)S(1)} %bitcast.29), channel_id=1, source_target_pairs={{0,1},{1,0},{2,3},{3,2},{4,5},{5,4},{6,7},{7,6},{8,9},{9,8},{10,11... | collective-permute-start | bytes 3145736 | tf_op jit(solution)/shard_map/ppermute | solution.py:94
  121.0 7.7 %collective-permute-start.20 = (bf16[4,64,512]{2,1,0:T(8,128)(2,1)S(1)}, bf16[4,64,512]{2,1,0:T(8,128)(2,1)S(1)}, u32[]{:S(2)}, u32[]{:S(2)}) collective-permute-start(bf16[4,64,512]{2,1,0:T(8,128)(2,1)S(1)} %get-tuple-element.218), channel_id=1, source_target_pairs={{0,4},{2,6},{4,0},{6,2},{8,12},{10,14},{12,8},{14,10},{16,20},{18,... | collective-permute-start | bytes 786440 | tf_op jit(solution)/shard_map/ppermute | solution.py:94
  121.6 8.0 %collective-permute-start.21 = (bf16[4,64,512]{2,1,0:T(8,128)(2,1)S(1)}, bf16[4,64,512]{2,1,0:T(8,128)(2,1)S(1)}, u32[]{:S(2)}, u32[]{:S(2)}) collective-permute-start(bf16[4,64,512]{2,1,0:T(8,128)(2,1)S(1)} %get-tuple-element.220), channel_id=1, source_target_pairs={{0,2},{2,0},{4,6},{6,4},{8,10},{10,8},{12,14},{14,12},{16,18},{18,... | collective-permute-start | bytes 786440 | tf_op jit(solution)/shard_map/ppermute | solution.py:94
  126.2 18.6 %collective-permute-start.26 = (bf16[2,4,64,256]{3,2,1,0:T(8,128)(2,1)S(1)}, bf16[2,4,64,256]{3,2,1,0:T(8,128)(2,1)S(1)}, u32[]{:S(2)}, u32[]{:S(2)}) collective-permute-start(bf16[2,4,64,256]{3,2,1,0:T(8,128)(2,1)S(1)} %get-tuple-element.231), channel_id=1, source_target_pairs={{0,2},{2,0},{4,6},{6,4},{8,10},{10,8},{12,14},{14,12},{16,18},{18,... | collective-permute-start | bytes 786440 | tf_op jit(solution)/shard_map/ppermute | solution.py:94
  127.2 17.6 %collective-permute-start.27 = (bf16[2,4,64,256]{3,2,1,0:T(8,128)(2,1)S(1)}, bf16[2,4,64,256]{3,2,1,0:T(8,128)(2,1)S(1)}, u32[]{:S(2)}, u32[]{:S(2)}) collective-permute-start(bf16[2,4,64,256]{3,2,1,0:T(8,128)(2,1)S(1)} %get-tuple-element.233), channel_id=1, source_target_pairs={{0,4},{2,6},{4,0},{6,2},{8,12},{10,14},{12,8},{14,10},{16,20},{18,... | collective-permute-start | bytes 786440 | tf_op jit(solution)/shard_map/ppermute | solution.py:94
  129.7 15.2 %collective-permute-start.23 = (bf16[160,512]{1,0:T(8,128)(2,1)S(1)}, bf16[160,512]{1,0:T(8,128)(2,1)S(1)}, u32[]{:S(2)}, u32[]{:S(2)}) collective-permute-start(bf16[160,512]{1,0:T(8,128)(2,1)S(1)} %get-tuple-element.227), channel_id=1, source_target_pairs={{0,8},{2,10},{4,12},{6,14},{8,0},{10,2},{12,4},{14,6},{16,24},{18,... | collective-permute-start | bytes 491528 | tf_op jit(solution)/shard_map/ppermute | solution.py:94
  130.9 14.0 %collective-permute-start.24 = (bf16[160,512]{1,0:T(8,128)(2,1)S(1)}, bf16[160,512]{1,0:T(8,128)(2,1)S(1)}, u32[]{:S(2)}, u32[]{:S(2)}) collective-permute-start(bf16[160,512]{1,0:T(8,128)(2,1)S(1)} %get-tuple-element.228), channel_id=1, source_target_pairs={{0,16},{2,18},{4,20},{6,22},{8,24},{10,26},{12,28},{14,30},{16,0},... | collective-permute-start | bytes 491528 | tf_op jit(solution)/shard_map/ppermute | solution.py:94
  132.8 12.1 %collective-permute-start.25 = (bf16[160,512]{1,0:T(8,128)(2,1)S(1)}, bf16[160,512]{1,0:T(8,128)(2,1)S(1)}, u32[]{:S(2)}, u32[]{:S(2)}) collective-permute-start(bf16[160,512]{1,0:T(8,128)(2,1)S(1)} %get-tuple-element.229), channel_id=1, source_target_pairs={{0,24},{2,26},{4,28},{6,30},{8,16},{10,18},{12,20},{14,22},{16,8},... | collective-permute-start | bytes 491528 | tf_op jit(solution)/shard_map/ppermute | solution.py:94
  145.0 16.4 %collective-permute-start.28 = (bf16[128,512]{1,0:T(8,128)(2,1)S(1)}, bf16[128,512]{1,0:T(8,128)(2,1)S(1)}, u32[]{:S(2)}, u32[]{:S(2)}) collective-permute-start(bf16[128,512]{1,0:T(8,128)(2,1)S(1)} %get-tuple-element.237.refs_0_), channel_id=1, source_target_pairs={{0,8},{2,10},{4,12},{6,14},{8,0},{10,2},{12,4},{14,6},{16,24},{18,... | collective-permute-start | bytes 393224 | tf_op jit(solution)/shard_map/ppermute | solution.py:94
  145.7 17.0 %collective-permute-start.29 = (bf16[128,512]{1,0:T(8,128)(2,1)S(1)}, bf16[128,512]{1,0:T(8,128)(2,1)S(1)}, u32[]{:S(2)}, u32[]{:S(2)}) collective-permute-start(bf16[128,512]{1,0:T(8,128)(2,1)S(1)} %get-tuple-element.237.refs_0_), channel_id=1, source_target_pairs={{0,16},{2,18},{4,20},{6,22},{8,24},{10,26},{12,28},{14,30},{16,0},... | collective-permute-start | bytes 393224 | tf_op jit(solution)/shard_map/ppermute | solution.py:94
  148.1 14.7 %collective-permute-start.30 = (bf16[128,512]{1,0:T(8,128)(2,1)S(1)}, bf16[128,512]{1,0:T(8,128)(2,1)S(1)}, u32[]{:S(2)}, u32[]{:S(2)}) collective-permute-start(bf16[128,512]{1,0:T(8,128)(2,1)S(1)} %get-tuple-element.237.refs_0_), channel_id=1, source_target_pairs={{0,24},{2,26},{4,28},{6,30},{8,16},{10,18},{12,20},{14,22},{16,8},... | collective-permute-start | bytes 393224 | tf_op jit(solution)/shard_map/ppermute | solution.py:94
  149.5 8.8 %collective-permute-start.31 = (bf16[4,64,256]{2,1,0:T(8,128)(2,1)S(1)}, bf16[4,64,256]{2,1,0:T(8,128)(2,1)S(1)}, u32[]{:S(2)}, u32[]{:S(2)}) collective-permute-start(bf16[4,64,256]{2,1,0:T(8,128)(2,1)S(1)} %get-tuple-element.240), channel_id=1, source_target_pairs={{0,4},{2,6},{4,0},{6,2},{8,12},{10,14},{12,8},{14,10},{16,20},{18,... | collective-permute-start | bytes 393224 | tf_op jit(solution)/shard_map/ppermute | solution.py:94
  150.8 7.5 %collective-permute-start.32 = (bf16[4,64,256]{2,1,0:T(8,128)(2,1)S(1)}, bf16[4,64,256]{2,1,0:T(8,128)(2,1)S(1)}, u32[]{:S(2)}, u32[]{:S(2)}) collective-permute-start(bf16[4,64,256]{2,1,0:T(8,128)(2,1)S(1)} %get-tuple-element.242), channel_id=1, source_target_pairs={{0,2},{2,0},{4,6},{6,4},{8,10},{10,8},{12,14},{14,12},{16,18},{18,... | collective-permute-start | bytes 393224 | tf_op jit(solution)/shard_map/ppermute | solution.py:94
  158.3 11.2 %collective-permute-start.35 = (bf16[64,512]{1,0:T(8,128)(2,1)S(1)}, bf16[64,512]{1,0:T(8,128)(2,1)S(1)}, u32[]{:S(2)}, u32[]{:S(2)}) collective-permute-start(bf16[64,512]{1,0:T(8,128)(2,1)S(1)} %get-tuple-element.254), channel_id=1, source_target_pairs={{0,8},{2,10},{4,12},{6,14},{8,0},{10,2},{12,4},{14,6},{16,24},{18,... | collective-permute-start | bytes 196616 | tf_op jit(solution)/shard_map/ppermute | solution.py:94
  158.4 11.2 %collective-permute-start.36 = (bf16[64,512]{1,0:T(8,128)(2,1)S(1)}, bf16[64,512]{1,0:T(8,128)(2,1)S(1)}, u32[]{:S(2)}, u32[]{:S(2)}) collective-permute-start(bf16[64,512]{1,0:T(8,128)(2,1)S(1)} %get-tuple-element.255), channel_id=1, source_target_pairs={{0,16},{2,18},{4,20},{6,22},{8,24},{10,26},{12,28},{14,30},{16,0},... | collective-permute-start | bytes 196616 | tf_op jit(solution)/shard_map/ppermute | solution.py:94
  161.4 8.2 %collective-permute-start.37 = (bf16[64,512]{1,0:T(8,128)(2,1)S(1)}, bf16[64,512]{1,0:T(8,128)(2,1)S(1)}, u32[]{:S(2)}, u32[]{:S(2)}) collective-permute-start(bf16[64,512]{1,0:T(8,128)(2,1)S(1)} %get-tuple-element.256), channel_id=1, source_target_pairs={{0,24},{2,26},{4,28},{6,30},{8,16},{10,18},{12,20},{14,22},{16,8},... | collective-permute-start | bytes 196616 | tf_op jit(solution)/shard_map/ppermute | solution.py:94
  162.8 7.1 %collective-permute-start.34 = (bf16[4,80,512]{2,1,0:T(8,128)(2,1)S(1)}, bf16[4,80,512]{2,1,0:T(8,128)(2,1)S(1)}, u32[]{:S(2)}, u32[]{:S(2)}) collective-permute-start(bf16[4,80,512]{2,1,0:T(8,128)(2,1)S(1)} %get-tuple-element.252.refs_2_), channel_id=1, source_target_pairs={{0,2},{2,0},{4,6},{6,4},{8,10},{10,8},{12,14},{14,12},{16,18},{18,... | collective-permute-start | bytes 983048 | tf_op jit(solution)/shard_map/ppermute | solution.py:94
  163.1 6.5 %collective-permute-start.33 = (bf16[4,64,512]{2,1,0:T(8,128)(2,1)S(1)}, bf16[4,64,512]{2,1,0:T(8,128)(2,1)S(1)}, u32[]{:S(2)}, u32[]{:S(2)}) collective-permute-start(bf16[4,64,512]{2,1,0:T(8,128)(2,1)S(1)} %get-tuple-element.251.refs_0_), channel_id=1, source_target_pairs={{0,4},{2,6},{4,0},{6,2},{8,12},{10,14},{12,8},{14,10},{16,20},{18,... | collective-permute-start | bytes 786440 | tf_op jit(solution)/shard_map/ppermute | solution.py:94
  169.5 14.5 %collective-permute-start.45 = (f32[512,256]{1,0:T(8,128)S(1)}, f32[512,256]{1,0:T(8,128)S(1)}, u32[]{:S(2)}, u32[]{:S(2)}) collective-permute-start(f32[512,256]{1,0:T(8,128)S(1)} %get-tuple-element.265.refs_0_), channel_id=1, source_target_pairs={{0,1},{1,0},{2,3},{3,2},{4,5},{5,4},{6,7},{7,6},{8,9},{9,8},{10,11... | collective-permute-start | bytes 1572872 | tf_op jit(solution)/shard_map/ppermute | solution.py:94
  170.0 19.7 %collective-permute-start.39 = (bf16[2,4,80,512]{3,2,1,0:T(8,128)(2,1)S(1)}, bf16[2,4,80,512]{3,2,1,0:T(8,128)(2,1)S(1)}, u32[]{:S(2)}, u32[]{:S(2)}) collective-permute-start(bf16[2,4,80,512]{3,2,1,0:T(8,128)(2,1)S(1)} %get-tuple-element.260.refs_2_), channel_id=1, source_target_pairs={{0,4},{2,6},{4,0},{6,2},{8,12},{10,14},{12,8},{14,10},{16,20},{18,... | collective-permute-start | bytes 1966088 | tf_op jit(solution)/shard_map/ppermute | solution.py:94
  171.1 4.8 %collective-permute-start.40 = (bf16[64,512]{1,0:T(8,128)(2,1)S(1)}, bf16[64,512]{1,0:T(8,128)(2,1)S(1)}, u32[]{:S(2)}, u32[]{:S(2)}) collective-permute-start(bf16[64,512]{1,0:T(8,128)(2,1)S(1)} %get-tuple-element.261.refs_0_), channel_id=1, source_target_pairs={{0,8},{2,10},{4,12},{6,14},{8,0},{10,2},{12,4},{14,6},{16,24},{18,... | collective-permute-start | bytes 196616 | tf_op jit(solution)/shard_map/ppermute | solution.py:94
  171.5 18.3 %collective-permute-start.38 = (bf16[2,4,64,512]{3,2,1,0:T(8,128)(2,1)S(1)}, bf16[2,4,64,512]{3,2,1,0:T(8,128)(2,1)S(1)}, u32[]{:S(2)}, u32[]{:S(2)}) collective-permute-start(bf16[2,4,64,512]{3,2,1,0:T(8,128)(2,1)S(1)} %get-tuple-element.259.refs_0_), channel_id=1, source_target_pairs={{0,2},{2,0},{4,6},{6,4},{8,10},{10,8},{12,14},{14,12},{16,18},{18,... | collective-permute-start | bytes 1572872 | tf_op jit(solution)/shard_map/ppermute | solution.py:94
  172.9 7.9 %collective-permute-start.41 = (bf16[64,512]{1,0:T(8,128)(2,1)S(1)}, bf16[64,512]{1,0:T(8,128)(2,1)S(1)}, u32[]{:S(2)}, u32[]{:S(2)}) collective-permute-start(bf16[64,512]{1,0:T(8,128)(2,1)S(1)} %get-tuple-element.261.refs_0_), channel_id=1, source_target_pairs={{0,16},{2,18},{4,20},{6,22},{8,24},{10,26},{12,28},{14,30},{16,0},... | collective-permute-start | bytes 196616 | tf_op jit(solution)/shard_map/ppermute | solution.py:94
  175.9 6.2 %collective-permute-start.42 = (bf16[64,512]{1,0:T(8,128)(2,1)S(1)}, bf16[64,512]{1,0:T(8,128)(2,1)S(1)}, u32[]{:S(2)}, u32[]{:S(2)}) collective-permute-start(bf16[64,512]{1,0:T(8,128)(2,1)S(1)} %get-tuple-element.261.refs_0_), channel_id=1, source_target_pairs={{0,24},{2,26},{4,28},{6,30},{8,16},{10,18},{12,20},{14,22},{16,8},... | collective-permute-start | bytes 196616 | tf_op jit(solution)/shard_map/ppermute | solution.py:94
  182.1 7.6 %collective-permute-start.43 = (bf16[4,64,256]{2,1,0:T(8,128)(2,1)S(1)}, bf16[4,64,256]{2,1,0:T(8,128)(2,1)S(1)}, u32[]{:S(2)}, u32[]{:S(2)}) collective-permute-start(bf16[4,64,256]{2,1,0:T(8,128)(2,1)S(1)} %get-tuple-element.263.refs_0_), channel_id=1, source_target_pairs={{0,4},{2,6},{4,0},{6,2},{8,12},{10,14},{12,8},{14,10},{16,20},{18,... | collective-permute-start | bytes 393224 | tf_op jit(solution)/shard_map/ppermute | solution.py:94
  182.7 7.0 %collective-permute-start.44 = (bf16[4,64,256]{2,1,0:T(8,128)(2,1)S(1)}, bf16[4,64,256]{2,1,0:T(8,128)(2,1)S(1)}, u32[]{:S(2)}, u32[]{:S(2)}) collective-permute-start(bf16[4,64,256]{2,1,0:T(8,128)(2,1)S(1)} %get-tuple-element.264.refs_2_), channel_id=1, source_target_pairs={{0,2},{2,0},{4,6},{6,4},{8,10},{10,8},{12,14},{14,12},{16,18},{18,... | collective-permute-start | bytes 393224 | tf_op jit(solution)/shard_map/ppermute | solution.py:94
  189.9 3.2 %collective-permute-start.47 = (bf16[2,2,4,64,512]{4,3,2,1,0:T(8,128)(2,1)S(1)}, bf16[2,2,4,64,512]{4,3,2,1,0:T(8,128)(2,1)S(1)}, u32[]{:S(2)}, u32[]{:S(2)}) collective-permute-start(bf16[2,2,4,64,512]{4,3,2,1,0:T(8,128)(2,1)S(1)} %get-tuple-element.270), channel_id=1, source_target_pairs={{0,1},{1,0},{2,3},{3,2},{4,5},{5,4},{6,7},{7,6},{8,9},{9,8},{10,11... | collective-permute-start | bytes 3145736 | tf_op jit(solution)/shard_map/ppermute | solution.py:94
  190.0 9.6 %collective-permute-start.48 = (bf16[2,4,64,256]{3,2,1,0:T(8,128)(2,1)S(1)}, bf16[2,4,64,256]{3,2,1,0:T(8,128)(2,1)S(1)}, u32[]{:S(2)}, u32[]{:S(2)}) collective-permute-start(bf16[2,4,64,256]{3,2,1,0:T(8,128)(2,1)S(1)} %get-tuple-element.276.refs_0_), channel_id=1, source_target_pairs={{0,2},{2,0},{4,6},{6,4},{8,10},{10,8},{12,14},{14,12},{16,18},{18,... | collective-permute-start | bytes 786440 | tf_op jit(solution)/shard_map/ppermute | solution.py:94
  191.4 8.4 %collective-permute-start.49 = (bf16[2,4,64,256]{3,2,1,0:T(8,128)(2,1)S(1)}, bf16[2,4,64,256]{3,2,1,0:T(8,128)(2,1)S(1)}, u32[]{:S(2)}, u32[]{:S(2)}) collective-permute-start(bf16[2,4,64,256]{3,2,1,0:T(8,128)(2,1)S(1)} %get-tuple-element.277.refs_2_), channel_id=1, source_target_pairs={{0,4},{2,6},{4,0},{6,2},{8,12},{10,14},{12,8},{14,10},{16,20},{18,... | collective-permute-start | bytes 786440 | tf_op jit(solution)/shard_map/ppermute | solution.py:94
  193.2 3.2 %collective-permute-start.46 = (bf16[2,2,4,80,512]{4,3,2,1,0:T(8,128)(2,1)S(1)}, bf16[2,2,4,80,512]{4,3,2,1,0:T(8,128)(2,1)S(1)}, u32[]{:S(2)}, u32[]{:S(2)}) collective-permute-start(bf16[2,2,4,80,512]{4,3,2,1,0:T(8,128)(2,1)S(1)} %get-tuple-element.269), channel_id=1, source_target_pairs={{0,1},{1,0},{2,3},{3,2},{4,5},{5,4},{6,7},{7,6},{8,9},{9,8},{10,11... | collective-permute-start | bytes 3932168 | tf_op jit(solution)/shard_map/ppermute | solution.py:94
  199.9 2.7 %collective-permute-start.50 = (bf16[2,2,4,64,512]{4,3,2,1,0:T(8,128)(2,1)S(1)}, bf16[2,2,4,64,512]{4,3,2,1,0:T(8,128)(2,1)S(1)}, u32[]{:S(2)}, u32[]{:S(2)}) collective-permute-start(bf16[2,2,4,64,512]{4,3,2,1,0:T(8,128)(2,1)S(1)} %get-tuple-element.279), channel_id=1, source_target_pairs={{0,1},{1,0},{2,3},{3,2},{4,5},{5,4},{6,7},{7,6},{8,9},{9,8},{10,11... | collective-permute-start | bytes 3145736 | tf_op jit(solution)/shard_map/ppermute | solution.py:94
  (10 other events, 17.6 us)
